TPU v7x, 512 devices: a whole 4x4x16 slice. The times are simulated.
512 devices in a mesh: dp: 32 (over y_hi, z), expert: 16 (over x, y_lo, core).
Axes of the slice: x: 4, y: 4 (y_hi: 2, y_lo: 2; y = y_hi * 2 + y_lo), z: 16, core: 2. Of those that a mesh axis runs over, the one named last changes fastest.
Arguments:
- images: bfloat16 [1536, 128, 640], P(('dp', 'expert')), may hold values from -24 to 24
- router: bfloat16 [640, 128], replicated, as said below
- w_in: bfloat16 [16, 640, 2560], P('expert', 'dp'), may hold values from -18 to 18, as said below
- w_out: bfloat16 [16, 2560, 640], P('expert', 'dp'), may hold values from -18 to 18, as said below
- history: float32 [16, 2, 16], P('expert'), may hold values from 2 to 8
- cotangent: bfloat16 [1536, 128, 640], P(('dp', 'expert')), may hold values from -6 to 6
Outputs:
- output: bfloat16 [1536, 128, 640], P(('dp', 'expert'))
- d_images: bfloat16 [1536, 128, 640], P(('dp', 'expert'))
- d_w_in: bfloat16 [16, 640, 2560], P('expert', 'dp')
- new_history: float32 [16, 2, 16], P('expert')
Inputs may be any that keep to these rules, and one draw needn't show every extreme that they name: `w_in`: of order one in the first of the 640 rows, growing linearly along the rows to several times that; scaled by scale_in. `w_out`: of order one in the first of the 2560 rows, growing linearly along the rows to several times that; scaled by scale_out. `router`: of order one over the square root of 640, or larger.
All inputs are finite; a program needn't handle non-finite values.
Results may differ from a plain program's by a relative error of at most 0.025.
Values may be sent and summed in bfloat16 or wider, within the bound.
No kernel may reach another device: no remote copies, remote signals or barrier semaphores. Data moves between devices by JAX's collectives and lax.ppermute only.
A program may use at most 64 MiB of HBM per device.

v0:
```python
import jax
import jax.numpy as jnp
from jax import lax
from jax.sharding import PartitionSpec as P


def gelu_back(pre_act, d_hidden):
    _, pullback = jax.vjp(jax.nn.gelu, pre_act)
    return pullback(d_hidden)[0]


def body(images, router, w_in, w_out, history, cotangent):
    width = images.shape[2]
    per_expert = router.shape[1] // lax.axis_size("expert")
    logits = jnp.einsum("bpd,ds->bps", images, router, preferred_element_type=jnp.float32)
    dispatch = jax.nn.softmax(logits, axis=1)
    combine = jax.nn.softmax(logits, axis=2)
    dispatch_batch = dispatch.astype(jnp.bfloat16)
    combine_b = combine.astype(jnp.bfloat16)
    slot_in = jnp.einsum(
        "bps,bpd->bsd", dispatch_batch, images, preferred_element_type=jnp.float32
    ).astype(jnp.bfloat16)
    routed = lax.all_to_all(slot_in, "expert", split_axis=1, concat_axis=0, tiled=True)
    rows_in = routed.reshape(-1, width)
    gathered_in, collected_output = (
        lax.all_gather(w_in, "dp", axis=1, tiled=True),
        lax.all_gather(w_out, "dp", axis=1, tiled=True),
    )
    scale_in = jnp.max(history[0, 0]) / 448.0
    scale_out = jnp.max(history[0, 1]) / 448.0
    pre_act = jnp.dot(rows_in, gathered_in[0], preferred_element_type=jnp.float32) * scale_in
    hidden = jax.nn.gelu(pre_act).astype(jnp.bfloat16)
    rows_out = (
        jnp.dot(hidden, collected_output[0], preferred_element_type=jnp.float32) * scale_out
    ).astype(jnp.bfloat16)
    returned = lax.all_to_all(
        rows_out.reshape(-1, per_expert, width), "expert", split_axis=0, concat_axis=1, tiled=True
    )
    output = jnp.einsum(
        "bps,bsd->bpd", combine_b, returned, preferred_element_type=jnp.float32
    ).astype(jnp.bfloat16)
    d_combine = jnp.einsum("bpd,bsd->bps", cotangent, returned, preferred_element_type=jnp.float32)
    d_slot_out = jnp.einsum(
        "bps,bpd->bsd", combine_b, cotangent, preferred_element_type=jnp.float32
    ).astype(jnp.bfloat16)
    routed_grad = lax.all_to_all(
        d_slot_out, "expert", split_axis=1, concat_axis=0, tiled=True
    ).reshape(-1, width)
    weight_in, weight_out = (gathered_in, collected_output)
    d_hidden = (
        lax.dot_general(
            routed_grad, weight_out[0], (((1,), (1,)), ((), ())), preferred_element_type=jnp.float32
        )
        * scale_out
    )
    d_pre = gelu_back(pre_act, d_hidden).astype(jnp.bfloat16)
    d_weight = lax.psum_scatter(
        (
            lax.dot_general(
                rows_in, d_pre, (((0,), (0,)), ((), ())), preferred_element_type=jnp.float32
            )
            * scale_in
        ).astype(jnp.bfloat16),
        "dp",
        scatter_dimension=0,
        tiled=True,
    )
    d_w_in = d_weight[None]
    d_rows = (
        lax.dot_general(
            d_pre, weight_in[0], (((1,), (1,)), ((), ())), preferred_element_type=jnp.float32
        )
        * scale_in
    ).astype(jnp.bfloat16)
    d_slot_in = lax.all_to_all(
        d_rows.reshape(-1, per_expert, width), "expert", split_axis=0, concat_axis=1, tiled=True
    )
    d_dispatch = jnp.einsum("bpd,bsd->bps", images, d_slot_in, preferred_element_type=jnp.float32)
    d_logits = dispatch * (d_dispatch - jnp.sum(dispatch * d_dispatch, axis=1, keepdims=True))
    d_logits = d_logits + combine * (
        d_combine - jnp.sum(combine * d_combine, axis=2, keepdims=True)
    )
    d_logits = d_logits.astype(jnp.bfloat16)
    d_images = jnp.einsum(
        "bps,bsd->bpd", dispatch_batch, d_slot_in, preferred_element_type=jnp.float32
    )
    d_images = d_images + jnp.einsum(
        "bps,ds->bpd", d_logits, router, preferred_element_type=jnp.float32
    )
    d_images = d_images.astype(jnp.bfloat16)
    local_in = jnp.max(jnp.abs(w_in)).astype(jnp.float32)
    local_out = jnp.max(jnp.abs(w_out)).astype(jnp.float32)
    peak_in, peak_out = lax.pmax((local_in, local_out), "dp")
    peaks = jnp.stack([peak_in, peak_out])
    new_history = jnp.concatenate([peaks[:, None], history[0, :, :-1]], axis=1)[None]
    return (output, d_images, d_w_in, new_history)


def solution(mesh):
    return jax.shard_map(
        body,
        mesh=mesh,
        in_specs=(
            P(("dp", "expert"), None, None),
            P(),
            P("expert", "dp", None),
            P("expert", "dp", None),
            P("expert", None, None),
            P(("dp", "expert"), None, None),
        ),
        out_specs=(
            P(("dp", "expert"), None, None),
            P(("dp", "expert"), None, None),
            P("expert", "dp", None),
            P("expert", None, None),
        ),
        check_vma=False,
    )
```

profile of v0, /device:TPU:1, one launch (start us, length us, event | category | flops | bytes accessed | tf_op | source)
XLA Modules:
  0.0 544.5 jit_solution(4676993972928079752)
XLA Ops:
  7.2 1.8 copy.37
  11.9 2.0 convolution_convert_fusion
  13.9 1.3 copy.40
  15.1 10.3 %all-to-all-start.2 = ((bf16[3,128,640]{2,0,1:T(4,128)(2,1)}), bf16[3,128,640]{2,0,1:T(4,128)(2,1)S(1)}, u32[]{:S(2)}, u32[]{:S(2)}) async-start(bf16[3,128,640]{2,0,1:T(4,128)(2,1)} %copy.40), calls=%async_computation.2 | async-start | bytes 1310720 | tf_op jit(solution)/shard_map/all_to_all | solution.py:46
  26.7 68.3 %all-reduce.2 = (f32[1]{0:T(128)}, f32[1]{0:T(128)}) all-reduce(bf16[1]{0:T(256)(128)(2,1)} %bitcast.30, bf16[1]{0:T(256)(128)(2,1)} %bitcast.29), channel_id=1, replica_groups=mesh['dp'=32,'expert'=16] {'dp'}, use_global_device_ids=true, to_apply=%region_12.0 | all-reduce | flops 2 | bytes 12 | tf_op jit(solution)/shard_map/pmax | solution.py:93
  96.1 1.3 copy.34
  97.3 19.2 %all-to-all-start = ((bf16[3,128,640]{2,0,1:T(4,128)(2,1)}), bf16[3,128,640]{2,0,1:T(4,128)(2,1)S(1)}, u32[]{:S(2)}, u32[]{:S(2)}) async-start(bf16[3,128,640]{2,0,1:T(4,128)(2,1)} %copy.34), calls=%async_computation | async-start | bytes 1310720 | tf_op jit(solution)/shard_map/all_to_all | solution.py:23
  116.6 1.3 maximum_bitcast_fusion.1
  119.9 1.3 dynamic-slice.4
  122.6 5.9 %all-to-all-done = bf16[3,128,640]{2,0,1:T(4,128)(2,1)S(1)} async-done(((bf16[3,128,640]{2,0,1:T(4,128)(2,1)}), bf16[3,128,640]{2,0,1:T(4,128)(2,1)S(1)}, u32[]{:S(2)}, u32[]{:S(2)}) %all-to-all-start) | async-done | bytes 491552 | tf_op jit(solution)/shard_map/all_to_all | solution.py:23
  128.6 66.6 %all-gather.3.cloned.1.call-done = bf16[1,640,2560]{2,0,1:T(2,128)(2,1)} async-done(((bf16[1,20,2560]{2,0,1:T(2,128)(2,1)}), bf16[1,640,2560]{2,0,1:T(2,128)(2,1)}) %all-gather.3.cloned.1.call-update) | async-done | bytes 3276816 | tf_op jit(solution)/shard_map/all_gather | solution.py:26
  195.1 6.5 %convolution_multiply_fusion.1 = f32[384,2560]{1,0:T(8,128)} fusion(bf16[384,640]{1,0:T(8,128)(2,1)S(1)} %bitcast.101, f32[]{:T(128)S(6)} %div.26, bf16[1,640,2560]{2,0,1:T(2,128)(2,1)} %all-gather.3.cloned.1.call-done), kind=kOutput, calls=%fused_computation.8 | convolution fusion | flops 1259274240 | bytes 7700484 | tf_op jit(solution)/shard_map/dot_general | solution.py:31
  201.6 147.0 %all-gather.5.cloned.1.call-done = bf16[1,2560,640]{2,1,0:T(8,128)(2,1)} async-done(((bf16[1,80,640]{2,1,0:T(8,128)(2,1)}), bf16[1,2560,640]{2,1,0:T(8,128)(2,1)}) %all-gather.5.cloned.1.call-update) | async-done | bytes 3276816 | tf_op jit(solution)/shard_map/all_gather | solution.py:27
  348.6 6.4 %fusion.11 = bf16[384,2560]{1,0:T(8,128)(2,1)S(1)} fusion(f32[384,2560]{1,0:T(8,128)} %convolution_multiply_fusion.1, bf16[384,640]{1,0:T(8,128)(2,1)S(1)} %bitcast.100, bf16[1,2560,640]{2,1,0:T(8,128)(2,1)} %all-gather.5.cloned.1.call-done, f32[]{:T(128)S(6)} %div.27), kind=kOutput, calls=%fused_computation.15 | convolution fusion | flops 1278935040 | bytes 9666564 | tf_op jit(solution)/shard_map/dot_general | solution.py:51
  355.1 1.3 copy-done.6
  356.4 3.6 multiply_convert_fusion
  360.0 81.8 %fusion = bf16[24,2560]{1,0:T(8,128)(2,1)S(1)} fusion(bf16[640,2560]{1,0:T(8,128)(2,1)} %multiply_convert_fusion), kind=kCustom, calls=%all-reduce-scatter | all-reduce-scatter fusion | flops 1966081 | bytes 3401728
  441.8 1.3 collective-permute-start.4
  443.1 1.3 collective-permute-start.3
  444.4 3.5 collective-permute-start.2
  447.9 5.5 %collective-permute-start.1 = (bf16[24,2560]{1,0:T(8,128)(2,1)S(1)}, bf16[24,2560]{1,0:T(8,128)(2,1)S(1)}, u32[]{:S(2)}, u32[]{:S(2)}) collective-permute-start(bf16[24,2560]{1,0:T(8,128)(2,1)S(1)} %fusion), channel_id=1, source_target_pairs={{0,32},{16,48},{32,64},{48,80},{64,96},{80,112},{96,128},{112,144}... | collective-permute-start | bytes 368648
  453.4 10.0 %collective-permute-start.5 = (bf16[4,2560]{1,0:T(4,128)(2,1)S(1)}, bf16[4,2560]{1,0:T(4,128)(2,1)S(1)}, u32[]{:S(2)}, u32[]{:S(2)}) collective-permute-start(bf16[4,2560]{1,0:T(4,128)(2,1)S(1)} %slice.12), channel_id=1, source_target_pairs={{0,96},{16,112},{32,128},{48,144},{64,160},{80,176},{96,192},{112,... | collective-permute-start | bytes 61448
  463.5 6.3 %fusion.40 = bf16[48,8,640]{2,1,0:T(8,128)(2,1)} fusion(bf16[1,2560,640]{2,1,0:T(8,128)(2,1)} %all-gather.5.cloned.1.call-done, f32[384,2560]{1,0:T(8,128)} %convolution_multiply_fusion.1, f32[]{:T(128)S(6)} %div.27), kind=kOutput, calls=%fused_computation.39 | convolution fusion | flops 1267630080 | bytes 7700484 | tf_op jit(solution)/shard_map/dot_general | solution.py:34
  469.8 36.2 %all-to-all-start.1 = ((bf16[48,8,640]{2,1,0:T(8,128)(2,1)}), bf16[48,8,640]{2,1,0:T(8,128)(2,1)S(1)}, u32[]{:S(2)}, u32[]{:S(2)}) async-start(bf16[48,8,640]{2,1,0:T(8,128)(2,1)} %fusion.40), calls=%async_computation.1 | async-start | bytes 983040 | tf_op jit(solution)/shard_map/all_to_all | solution.py:36
  505.9 2.4 collective-permute-start
  508.3 6.0 %fusion.37 = bf16[48,8,640]{2,1,0:T(8,128)(2,1)} fusion(bf16[384,2560]{1,0:T(8,128)(2,1)} %copy-done.6, bf16[1,640,2560]{2,0,1:T(2,128)(2,1)} %all-gather.3.cloned.1.call-done, f32[]{:T(128)S(6)} %div.26), kind=kOutput, calls=%fused_computation.38 | convolution fusion | flops 1258782720 | bytes 5734404 | tf_op jit(solution)/shard_map/dot_general | solution.py:70
  514.3 1.3 concatenate.4
  516.4 6.0 %all-to-all-start.3 = ((bf16[48,8,640]{2,1,0:T(8,128)(2,1)}), bf16[48,8,640]{2,1,0:T(8,128)(2,1)S(1)}, u32[]{:S(2)}, u32[]{:S(2)}) async-start(bf16[48,8,640]{2,1,0:T(8,128)(2,1)} %fusion.37), calls=%async_computation.3 | async-start | bytes 983040 | tf_op jit(solution)/shard_map/all_to_all | solution.py:75
  522.4 1.6 convolution_convert_fusion.1
  525.0 6.8 %all-to-all-done.3 = bf16[48,8,640]{2,1,0:T(8,128)(2,1)S(1)} async-done(((bf16[48,8,640]{2,1,0:T(8,128)(2,1)}), bf16[48,8,640]{2,1,0:T(8,128)(2,1)S(1)}, u32[]{:S(2)}, u32[]{:S(2)}) %all-to-all-start.3) | async-done | bytes 491552 | tf_op jit(solution)/shard_map/all_to_all | solution.py:75
  532.4 3.2 fusion.49
  535.6 2.1 fusion.31
  (44 shorter events, 9.1 us)
Async XLA Ops:
  7.2 2.7 copy-start
  7.2 18.8 %copy-start.3 = (bf16[1,20,2560]{2,1,0:T(8,128)(2,1)S(1)}, bf16[1,20,2560]{2,1,0:T(8,128)(2,1)}, u32[]{:S(2)}) copy-start(bf16[1,20,2560]{2,1,0:T(8,128)(2,1)} %param.8) | copy-start | bytes 307204
  7.2 18.2 %copy-start.4 = (bf16[1,80,640]{2,1,0:T(8,128)(2,1)S(1)}, bf16[1,80,640]{2,1,0:T(8,128)(2,1)}, u32[]{:S(2)}) copy-start(bf16[1,80,640]{2,1,0:T(8,128)(2,1)} %param.9) | copy-start | bytes 307204
  7.2 187.9 %all-gather.3.cloned.1.call-start = ((), (), s32[]{:S(2)}) async-start(), calls=%async_computation.4 | async-start | bytes 6758400 | tf_op jit(solution)/shard_map/all_gather | solution.py:26
  9.1 339.6 %all-gather.5.cloned.1.call-start = ((), (), s32[]{:S(2)}) async-start(), calls=%async_computation.5 | async-start | bytes 3379200 | tf_op jit(solution)/shard_map/all_gather | solution.py:27
  11.9 106.1 %copy-start.5 = (f32[1,2,16]{2,1,0:T(2,128)S(1)}, f32[1,2,16]{2,1,0:T(2,128)}, u32[]{:S(2)}) copy-start(f32[1,2,16]{2,1,0:T(2,128)} %param.10) | copy-start | bytes 388
  15.1 82.2 %all-to-all-start.2 = ((bf16[3,128,640]{2,0,1:T(4,128)(2,1)}), bf16[3,128,640]{2,0,1:T(4,128)(2,1)S(1)}, u32[]{:S(2)}, u32[]{:S(2)}) async-start(bf16[3,128,640]{2,0,1:T(4,128)(2,1)} %copy.40), calls=%async_computation.2 | async-start | bytes 1310720 | tf_op jit(solution)/shard_map/all_to_all | solution.py:46
  97.3 31.1 %all-to-all-start = ((bf16[3,128,640]{2,0,1:T(4,128)(2,1)}), bf16[3,128,640]{2,0,1:T(4,128)(2,1)S(1)}, u32[]{:S(2)}, u32[]{:S(2)}) async-start(bf16[3,128,640]{2,0,1:T(4,128)(2,1)} %copy.34), calls=%async_computation | async-start | bytes 1310720 | tf_op jit(solution)/shard_map/all_to_all | solution.py:23
  355.1 1.3 copy-start.6
  441.8 72.5 %collective-permute-start.4 = (bf16[24,2560]{1,0:T(8,128)(2,1)S(1)}, bf16[24,2560]{1,0:T(8,128)(2,1)S(1)}, u32[]{:S(2)}, u32[]{:S(2)}) collective-permute-start(bf16[24,2560]{1,0:T(8,128)(2,1)S(1)} %fusion), channel_id=1, source_target_pairs={{0,80},{16,96},{32,112},{48,128},{64,144},{80,160},{96,176},{112,1... | collective-permute-start | bytes 368648
  443.1 71.2 %collective-permute-start.3 = (bf16[24,2560]{1,0:T(8,128)(2,1)S(1)}, bf16[24,2560]{1,0:T(8,128)(2,1)S(1)}, u32[]{:S(2)}, u32[]{:S(2)}) collective-permute-start(bf16[24,2560]{1,0:T(8,128)(2,1)S(1)} %fusion), channel_id=1, source_target_pairs={{0,64},{16,80},{32,96},{48,112},{64,128},{80,144},{96,160},{112,17... | collective-permute-start | bytes 368648
  444.4 69.9 %collective-permute-start.2 = (bf16[24,2560]{1,0:T(8,128)(2,1)S(1)}, bf16[24,2560]{1,0:T(8,128)(2,1)S(1)}, u32[]{:S(2)}, u32[]{:S(2)}) collective-permute-start(bf16[24,2560]{1,0:T(8,128)(2,1)S(1)} %fusion), channel_id=1, source_target_pairs={{0,48},{16,64},{32,80},{48,96},{64,112},{80,128},{96,144},{112,160... | collective-permute-start | bytes 368648
  447.9 66.4 %collective-permute-start.1 = (bf16[24,2560]{1,0:T(8,128)(2,1)S(1)}, bf16[24,2560]{1,0:T(8,128)(2,1)S(1)}, u32[]{:S(2)}, u32[]{:S(2)}) collective-permute-start(bf16[24,2560]{1,0:T(8,128)(2,1)S(1)} %fusion), channel_id=1, source_target_pairs={{0,32},{16,48},{32,64},{48,80},{64,96},{80,112},{96,128},{112,144}... | collective-permute-start | bytes 368648
  453.4 52.5 %collective-permute-start.5 = (bf16[4,2560]{1,0:T(4,128)(2,1)S(1)}, bf16[4,2560]{1,0:T(4,128)(2,1)S(1)}, u32[]{:S(2)}, u32[]{:S(2)}) collective-permute-start(bf16[4,2560]{1,0:T(4,128)(2,1)S(1)} %slice.12), channel_id=1, source_target_pairs={{0,96},{16,112},{32,128},{48,144},{64,160},{80,176},{96,192},{112,... | collective-permute-start | bytes 61448
  469.8 46.6 %all-to-all-start.1 = ((bf16[48,8,640]{2,1,0:T(8,128)(2,1)}), bf16[48,8,640]{2,1,0:T(8,128)(2,1)S(1)}, u32[]{:S(2)}, u32[]{:S(2)}) async-start(bf16[48,8,640]{2,1,0:T(8,128)(2,1)} %fusion.40), calls=%async_computation.1 | async-start | bytes 983040 | tf_op jit(solution)/shard_map/all_to_all | solution.py:36
  505.9 8.4 %collective-permute-start = (bf16[24,2560]{1,0:T(8,128)(2,1)S(1)}, bf16[24,2560]{1,0:T(8,128)(2,1)S(1)}, u32[]{:S(2)}, u32[]{:S(2)}) collective-permute-start(bf16[24,2560]{1,0:T(8,128)(2,1)S(1)} %fusion), channel_id=1, source_target_pairs={{0,16},{16,32},{32,48},{48,64},{64,80},{80,96},{96,112},{112,128},... | collective-permute-start | bytes 368648
  514.3 9.7 %copy-start.2 = (bf16[3,128,640]{2,1,0:T(8,128)(2,1)S(1)}, bf16[3,128,640]{2,1,0:T(8,128)(2,1)}, u32[]{:S(2)}) copy-start(bf16[3,128,640]{2,1,0:T(8,128)(2,1)} %param.11) | copy-start | bytes 1474564
  515.7 19.9 %copy-start.1 = (bf16[640,128]{1,0:T(8,128)(2,1)S(1)}, bf16[640,128]{1,0:T(8,128)(2,1)}, u32[]{:S(2)}) copy-start(bf16[640,128]{1,0:T(8,128)(2,1)} %param.7) | copy-start | bytes 491524
  516.4 15.3 %all-to-all-start.3 = ((bf16[48,8,640]{2,1,0:T(8,128)(2,1)}), bf16[48,8,640]{2,1,0:T(8,128)(2,1)S(1)}, u32[]{:S(2)}, u32[]{:S(2)}) async-start(bf16[48,8,640]{2,1,0:T(8,128)(2,1)} %fusion.37), calls=%async_computation.3 | async-start | bytes 983040 | tf_op jit(solution)/shard_map/all_to_all | solution.py:75
Sparse Core Ops, SparseCore 0:
  11.7 183.3 all-gather.2
  198.2 150.3 all-gather.4
where the time goes:
time: 545 us
  waiting for transfers between devices  227 us (42%)
  blocking collectives  150 us (28%)
  starting transfers between devices  95.7 us (18%)
  matrix products  37.7 us (7%)
  between operations  16.2 us (3%)
  local copies, waits for them, and re-layouts  9.26 us (2%)
  other arithmetic  8.6 us (2%)
    all_gather x1, waiting for transfers between devices, body(): lax.all_gather(w_out, 'dp', axis=1, tiled=True)  147 us
    unnamed x1, blocking collectives  81.8 us
    pmax x1, blocking collectives, body(): peak_in, peak_out = lax.pmax((local_in, local_out), 'dp')  68.3 us
    all_gather x1, waiting for transfers between devices, body(): lax.all_gather(w_in, 'dp', axis=1, tiled=True)  66.6 us
    all_to_all x1, starting transfers between devices, body(): lax.all_to_all(rows_out.reshape(-1, per_expert, width), 'expert', split_a...  36.2 us
    unnamed x6, starting transfers between devices  24 us
    all_to_all x1, starting transfers between devices, body(): lax.all_to_all(slot_in, 'expert', split_axis=1, concat_axis=0, tiled=True)  19.2 us
  transfers between devices with their start and end apart: 12, of which 4 were waited for; matrix products, arithmetic and copies ran while one was open for 7% of the time, Pallas kernels for 0%

commit v1 on v0

v1 whole, which is shorter than its diff:
```python
import jax
import jax.numpy as jnp
import numpy as np
from jax import lax
from jax.experimental import pallas as pl
from jax.experimental.pallas import tpu as pltpu
from jax.sharding import Mesh
from jax.sharding import PartitionSpec as P

PAD = 48
CHUNK = 640
C0 = 0.7978845608028654
C1 = 0.044715


def expert_kernel(scale_ref, rows_ref, grad_ref, w_in_ref, w_out_ref, dw_ref, out_ref, drow_ref, out_acc, drow_acc):
    step = pl.program_id(0)
    scale_in = scale_ref[0]
    scale_out = scale_ref[1]
    rows = rows_ref[...]
    grad = grad_ref[...]
    w_in = w_in_ref[...].reshape(rows.shape[1], -1)
    w_out = w_out_ref[...].reshape(-1, grad.shape[1])
    pre = jnp.dot(rows, w_in, preferred_element_type=jnp.float32) * scale_in
    d_hidden = (
        lax.dot_general(grad, w_out, (((1,), (1,)), ((), ())), preferred_element_type=jnp.float32)
        * scale_out
    )
    square = pre * pre
    tanh = jnp.tanh(C0 * (pre + C1 * (square * pre)))
    half = 0.5 * (1.0 + tanh)
    hidden = (pre * half).astype(jnp.bfloat16)
    slope = half + (0.5 * C0) * pre * (1.0 - tanh * tanh) * (1.0 + (3.0 * C1) * square)
    d_pre = (slope * d_hidden).astype(jnp.bfloat16)
    dw = lax.dot_general(rows, d_pre, (((0,), (0,)), ((), ())), preferred_element_type=jnp.float32)
    dw_ref[...] = (dw * scale_in).astype(dw_ref.dtype)
    out = jnp.dot(hidden, w_out, preferred_element_type=jnp.float32)
    drow = lax.dot_general(d_pre, w_in, (((1,), (1,)), ((), ())), preferred_element_type=jnp.float32)

    @pl.when(step == 0)
    def _():
        out_acc[...] = out
        drow_acc[...] = drow

    @pl.when(step > 0)
    def _():
        out_acc[...] += out
        drow_acc[...] += drow

    @pl.when(step == pl.num_programs(0) - 1)
    def _():
        out_ref[...] = (out_acc[...] * scale_out).astype(out_ref.dtype)
        drow_ref[...] = (drow_acc[...] * scale_in).astype(drow_ref.dtype)


def experts(scales, rows, grads, weights):
    count, depth = rows.shape
    width = grads.shape[1]
    zs = weights.shape[0]
    chunks = 4
    return pl.pallas_call(
        expert_kernel,
        grid=(chunks,),
        in_specs=[
            pl.BlockSpec(memory_space=pltpu.SMEM),
            pl.BlockSpec((count, depth), lambda r: (0, 0)),
            pl.BlockSpec((count, width), lambda r: (0, 0)),
            pl.BlockSpec((zs, PAD, CHUNK), lambda r: (0, 4 + r, 0)),
            pl.BlockSpec((zs // 2, 80, width), lambda r: (r % 2, r // 2, 0)),
        ],
        out_specs=[
            pl.BlockSpec((depth, CHUNK), lambda r: (0, r)),
            pl.BlockSpec((count, width), lambda r: (0, 0)),
            pl.BlockSpec((count, depth), lambda r: (0, 0)),
        ],
        out_shape=[
            jax.ShapeDtypeStruct((depth, chunks * CHUNK), jnp.bfloat16),
            jax.ShapeDtypeStruct((count, width), jnp.bfloat16),
            jax.ShapeDtypeStruct((count, depth), jnp.bfloat16),
        ],
        scratch_shapes=[
            pltpu.VMEM((count, width), jnp.float32),
            pltpu.VMEM((count, depth), jnp.float32),
        ],
        compiler_params=pltpu.CompilerParams(vmem_limit_bytes=40 * 1024 * 1024),
        cost_estimate=pl.CostEstimate(
            flops=10 * count * width * chunks * CHUNK,
            bytes_accessed=16 * 1024 * 1024,
            transcendentals=count * chunks * CHUNK,
        ),
    )(scales, rows, grads, weights, weights)


def placement(width, zs):
    per = width // (2 * zs)
    table = np.zeros((width, zs * PAD), np.float32)
    for half in range(2):
        for z in range(zs):
            for i in range(per):
                table[(half * zs + z) * per + i, z * PAD + half * per + i] = 1.0
    return table


def body(images, router, w_in, w_out, history, cotangent):
    bf16 = jnp.bfloat16
    f32 = jnp.float32
    width = images.shape[2]
    count = images.shape[0]
    zs = lax.axis_size("z")
    n_expert = lax.axis_size("x") * lax.axis_size("yl") * lax.axis_size("c")
    per_expert = router.shape[1] // n_expert
    along = ("x", "yl", "c")
    half = lax.axis_index("yh")

    local_out = w_out[0]
    local_in = w_in[0]
    mine = jnp.concatenate([local_in.reshape(20, 4, CHUNK).transpose(1, 0, 2).reshape(80, CHUNK), local_out], 0)
    other = lax.ppermute(mine, "yh", [(0, 1), (1, 0)])
    low = jnp.where(half == 0, mine, other)
    high = jnp.where(half == 0, other, mine)
    gap = jnp.zeros((4, PAD - 40, CHUNK), bf16)
    in_part = jnp.concatenate(
        [low[:80].reshape(4, 20, CHUNK), high[:80].reshape(4, 20, CHUNK), gap], 1
    ).reshape(4 * PAD, CHUNK)
    out_part = jnp.concatenate([low[80:], high[80:]], 0)
    peak_in = jnp.full((16, CHUNK), jnp.max(jnp.abs(in_part)))
    peak_out = jnp.full((16, CHUNK), jnp.max(jnp.abs(out_part)))
    block = jnp.concatenate([out_part, peak_in, peak_out, in_part], 0)
    weights = lax.all_gather(block, "z", axis=0, tiled=False)

    logits = jnp.einsum("bpd,ds->bps", images, router, preferred_element_type=f32)
    dispatch = jax.nn.softmax(logits, axis=1)
    combine = jax.nn.softmax(logits, axis=2)
    dispatch_b = dispatch.astype(bf16)
    combine_b = combine.astype(bf16)
    slot_in = jnp.einsum("bps,bpd->bsd", dispatch_b, images, preferred_element_type=f32).astype(bf16)
    d_slot_out = jnp.einsum("bps,bpd->bsd", combine_b, cotangent, preferred_element_type=f32).astype(bf16)
    both = jnp.stack([slot_in, d_slot_out]).reshape(2, count, n_expert, per_expert, width)
    both = both.transpose(2, 0, 1, 3, 4)
    routed = lax.all_to_all(both, along, split_axis=0, concat_axis=0, tiled=True)
    rows = routed[:, 0].reshape(-1, width)
    grads = routed[:, 1].reshape(-1, width)
    spread = jnp.asarray(placement(width, zs), bf16)
    rows = jnp.dot(rows, spread, preferred_element_type=f32).astype(bf16)

    scales = jnp.max(history[0], axis=1) / 448.0
    dw, rows_out, d_rows = experts(scales, rows, grads, weights)
    d_rows = lax.dot_general(
        d_rows, spread, (((1,), (1,)), ((), ())), preferred_element_type=f32
    ).astype(bf16)

    part = lax.psum_scatter(dw, "z", scatter_dimension=0, tiled=True)
    keep = jnp.where(half == 0, part[:20], part[20:40])
    send = jnp.where(half == 0, part[20:40], part[:20])
    got = lax.ppermute(send, "yh", [(0, 1), (1, 0)])
    d_w_in = (keep.astype(f32) + got.astype(f32)).astype(bf16)[None]

    back = jnp.stack(
        [rows_out.reshape(n_expert, -1, width), d_rows.reshape(n_expert, -1, width)], 1
    ).reshape(n_expert, 2, count, per_expert, width)
    returned = lax.all_to_all(back, along, split_axis=0, concat_axis=0, tiled=True)
    returned = returned.transpose(1, 2, 0, 3, 4).reshape(2, count, -1, width)
    slot_out = returned[0]
    d_slot_in = returned[1]
    output = jnp.einsum("bps,bsd->bpd", combine_b, slot_out, preferred_element_type=f32).astype(bf16)
    d_combine = jnp.einsum("bpd,bsd->bps", cotangent, slot_out, preferred_element_type=f32)
    d_dispatch = jnp.einsum("bpd,bsd->bps", images, d_slot_in, preferred_element_type=f32)
    d_logits = dispatch * (d_dispatch - jnp.sum(dispatch * d_dispatch, axis=1, keepdims=True))
    d_logits = d_logits + combine * (d_combine - jnp.sum(combine * d_combine, axis=2, keepdims=True))
    d_logits = d_logits.astype(bf16)
    d_images = jnp.einsum("bps,bsd->bpd", dispatch_b, d_slot_in, preferred_element_type=f32)
    d_images = d_images + jnp.einsum("bps,ds->bpd", d_logits, router, preferred_element_type=f32)
    d_images = d_images.astype(bf16)

    peaks = jnp.max(weights[:, 160:192:16, 0], axis=0).astype(f32)
    new_history = jnp.concatenate([peaks[:, None], history[0, :, :-1]], axis=1)[None]
    return (output, d_images, d_w_in, new_history)


def solution(mesh):
    fine = Mesh(mesh.devices.reshape(2, 16, 4, 2, 2), ("yh", "z", "x", "yl", "c"))
    dp = ("yh", "z")
    expert = ("x", "yl", "c")
    every = dp + expert
    return jax.shard_map(
        body,
        mesh=fine,
        in_specs=(
            P(every, None, None),
            P(),
            P(expert, dp, None),
            P(expert, dp, None),
            P(expert, None, None),
            P(every, None, None),
        ),
        out_specs=(
            P(every, None, None),
            P(every, None, None),
            P(expert, dp, None),
            P(expert, None, None),
        ),
        check_vma=False,
    )
```

time: 545 us -> 243 us (0.45)
  the two profiles are of different devices: /device:TPU:1 before, /device:TPU:12 now
where the time goes in v1:
time: 243 us
  waiting for transfers between devices  162 us (67%)
  starting transfers between devices  21.9 us (9%)
  between operations  14.3 us (6%)
  Pallas kernels  12.8 us (5%)
  other arithmetic  12.3 us (5%)
  local copies, waits for them, and re-layouts  11 us (5%)
  matrix products  8.75 us (4%)
    all_gather x1, waiting for transfers between devices, body(): weights = lax.all_gather(block, 'z', axis=0, tiled=False)  77.6 us
    reduce_scatter x1, waiting for transfers between devices, body(): part = lax.psum_scatter(dw, 'z', scatter_dimension=0, tiled=True)  50.8 us
    all_to_all x1, waiting for transfers between devices, body(): lax.all_to_all(both, along, split_axis=0, concat_axis=0, tiled=True)  12.9 us
    pallas_call x1, Pallas kernels, experts(): pl.pallas_call(expert_kernel, grid=(chunks,), in_specs=[pl.BlockSpec(memo...  12.8 us
    all_to_all x1, waiting for transfers between devices, body(): lax.all_to_all(back, along, split_axis=0, concat_axis=0, tiled=True)  11.3 us
    unnamed x22, local copies, waits for them, and re-layouts  8.5 us
    all_to_all x1, starting transfers between devices, body(): lax.all_to_all(both, along, split_axis=0, concat_axis=0, tiled=True)  8.2 us
    ppermute x1, waiting for transfers between devices, body(): other = lax.ppermute(mine, 'yh', [(0, 1), (1, 0)])  5.91 us
  transfers between devices with their start and end apart: 6, of which 6 were waited for; matrix products, arithmetic and copies ran while one was open for 7% of the time, Pallas kernels for 0%

profile of v1, /device:TPU:12, one launch (start us, length us, event | category | flops | bytes accessed | tf_op | source)
XLA Modules:
  0.0 242.7 jit_solution(15401611725542324024)
XLA Ops:
  7.2 1.0 reshape_squeeze.11
  8.3 0.9 pad_maximum_fusion.2
  9.2 4.2 %collective-permute-start = (bf16[160,640]{1,0:T(8,128)(2,1)S(1)}, bf16[160,640]{1,0:T(8,128)(2,1)S(1)}, u32[]{:S(2)}, u32[]{:S(2)}) collective-permute-start(bf16[160,640]{1,0:T(8,128)(2,1)S(1)} %pad_maximum_fusion.2), channel_id=1, source_target_pairs={{0,256},{256,0},{1,257},{257,1},{2,258},{258,2},{3,259},{259,3},{4... | collective-permute-start | bytes 614408 | tf_op jit(solution)/shard_map/ppermute | solution.py:118
  13.6 5.9 %collective-permute-done = bf16[160,640]{1,0:T(8,128)(2,1)S(1)} collective-permute-done((bf16[160,640]{1,0:T(8,128)(2,1)S(1)}, bf16[160,640]{1,0:T(8,128)(2,1)S(1)}, u32[]{:S(2)}, u32[]{:S(2)}) %collective-permute-start) | collective-permute-done | bytes 204832 | tf_op jit(solution)/shard_map/ppermute | solution.py:118
  19.5 1.0 broadcast_select_fusion
  20.6 0.7 abs_reduce_fusion
  22.6 0.7 constant_dynamic-update-slice_fusion.1
  23.3 0.8 copy-done.3
  24.4 0.8 fusion.44
  25.5 0.8 fusion.43
  26.4 0.9 fusion.6
  27.3 1.1 copy_bitcast_fusion
  28.4 8.2 %all-to-all-start = ((bf16[16,2,3,8,640]{4,3,2,1,0:T(8,128)(2,1)}), bf16[16,2,3,8,640]{4,3,2,1,0:T(8,128)(2,1)S(1)}, u32[]{:S(2)}, u32[]{:S(2)}) async-start(bf16[16,2,3,8,640]{4,3,2,1,0:T(8,128)(2,1)} %copy_bitcast_fusion), calls=%async_computation | async-start | bytes 1966080 | tf_op jit(solution)/shard_map/all_to_all | solution.py:140
  36.8 12.9 %all-to-all-done = bf16[16,2,3,8,640]{4,3,2,1,0:T(8,128)(2,1)S(1)} async-done(((bf16[16,2,3,8,640]{4,3,2,1,0:T(8,128)(2,1)}), bf16[16,2,3,8,640]{4,3,2,1,0:T(8,128)(2,1)S(1)}, u32[]{:S(2)}, u32[]{:S(2)}) %all-to-all-start) | async-done | bytes 983072 | tf_op jit(solution)/shard_map/all_to_all | solution.py:140
  49.8 1.8 convolution_convert_fusion.rows_ref
  51.7 77.6 %all-gather.3.cloned.1.call-done = bf16[6144,640]{1,0:T(8,128)(2,1)} async-done(((bf16[384,640]{1,0:T(8,128)(2,1)}), bf16[6144,640]{1,0:T(8,128)(2,1)}) %all-gather.3.cloned.1.call-update) | async-done | bytes 7864336 | tf_op jit(solution)/shard_map/all_gather | solution.py:129
  129.2 3.2 %copy-done.2 = bf16[6144,640]{1,0:T(8,128)(2,1)S(1)} copy-done((bf16[6144,640]{1,0:T(8,128)(2,1)S(1)}, bf16[6144,640]{1,0:T(8,128)(2,1)}, u32[]{:S(2)}) %copy-start.2) | copy-done | bytes 7864344
  132.5 12.8 %shard_map.102 = (bf16[768,2560]{1,0:T(8,128)(2,1)S(1)}, bf16[384,640]{1,0:T(8,128)(2,1)S(1)}, bf16[384,768]{1,0:T(8,128)(2,1)S(1)}) custom-call(f32[2]{0:T(128)S(1)} %broadcast_multiply_fusion.scale_ref, bf16[384,768]{1,0:T(8,128)(2,1)S(1)} %convolution_convert_fusion.rows_ref, bf16[384,640]{1,0:T(8,128)(2,1)S(1)} %bitcast.65, ...), custom_call_target="tpu_custom_call" | custom-call | flops 6291456000 | bytes 16777216 | tf_op jit(solution)/shard_map/pallas_call | solution.py:61
  145.3 2.0 copy-done.1
  147.3 1.2 copy-done.9
  149.2 1.1 pad_maximum_fusion.1
  150.3 5.7 %all-to-all-start.1 = ((bf16[16,2,3,8,640]{4,3,2,1,0:T(8,128)(2,1)}), bf16[16,2,3,8,640]{4,3,2,1,0:T(8,128)(2,1)S(1)}, u32[]{:S(2)}, u32[]{:S(2)}) async-start(bf16[16,2,3,8,640]{4,3,2,1,0:T(8,128)(2,1)} %pad_maximum_fusion.1), calls=%async_computation.1 | async-start | bytes 1966080 | tf_op jit(solution)/shard_map/all_to_all | solution.py:161
  156.0 1.0 slice.50
  157.9 11.3 %all-to-all-done.1 = bf16[16,2,3,8,640]{4,3,2,1,0:T(8,128)(2,1)S(1)} async-done(((bf16[16,2,3,8,640]{4,3,2,1,0:T(8,128)(2,1)}), bf16[16,2,3,8,640]{4,3,2,1,0:T(8,128)(2,1)S(1)}, u32[]{:S(2)}, u32[]{:S(2)}) %all-to-all-start.1) | async-done | bytes 983072 | tf_op jit(solution)/shard_map/all_to_all | solution.py:161
  169.6 1.7 fusion.13
  171.9 2.1 fusion.4
  174.0 50.8 %reduce-scatter.2.cloned.1.call-done = bf16[48,2560]{1,0:T(8,128)(2,1)} async-done(((bf16[768,2560]{1,0:T(8,128)(2,1)}), bf16[48,2560]{1,0:T(8,128)(2,1)}) %reduce-scatter.2.cloned.1.call-update) | async-done | bytes 245776 | tf_op jit(solution)/shard_map/reduce_scatter | solution.py:152
  224.8 1.0 broadcast_select_fusion.2
  225.9 3.7 %collective-permute-start.1 = (bf16[20,2560]{1,0:T(8,128)(2,1)S(1)}, bf16[20,2560]{1,0:T(8,128)(2,1)S(1)}, u32[]{:S(2)}, u32[]{:S(2)}) collective-permute-start(bf16[20,2560]{1,0:T(8,128)(2,1)S(1)} %broadcast_select_fusion.2), channel_id=1, source_target_pairs={{0,256},{256,0},{1,257},{257,1},{2,258},{258,2},{3,259},{259,3},{4... | collective-permute-start | bytes 307208 | tf_op jit(solution)/shard_map/ppermute | solution.py:155
  229.5 1.6 convolution_convert_fusion.1
  231.1 3.0 %collective-permute-done.1 = bf16[20,2560]{1,0:T(8,128)(2,1)S(1)} collective-permute-done((bf16[20,2560]{1,0:T(8,128)(2,1)S(1)}, bf16[20,2560]{1,0:T(8,128)(2,1)S(1)}, u32[]{:S(2)}, u32[]{:S(2)}) %collective-permute-start.1) | collective-permute-done | bytes 102432 | tf_op jit(solution)/shard_map/ppermute | solution.py:155
  234.1 1.7 fusion.33
  (46 shorter events, 5.1 us)
Async XLA Ops:
  7.2 16.9 %copy-start = (bf16[3,128,640]{2,1,0:T(8,128)(2,1)S(1)}, bf16[3,128,640]{2,1,0:T(8,128)(2,1)}, u32[]{:S(2)}) copy-start(bf16[3,128,640]{2,1,0:T(8,128)(2,1)} %param.7) | copy-start | bytes 1474564
  7.2 16.9 %copy-start.4 = (bf16[640,128]{1,0:T(8,128)(2,1)S(1)}, bf16[640,128]{1,0:T(8,128)(2,1)}, u32[]{:S(2)}) copy-start(bf16[640,128]{1,0:T(8,128)(2,1)} %param.8) | copy-start | bytes 491524
  7.2 19.2 %copy-start.5 = (bf16[3,128,640]{2,1,0:T(8,128)(2,1)S(1)}, bf16[3,128,640]{2,1,0:T(8,128)(2,1)}, u32[]{:S(2)}) copy-start(bf16[3,128,640]{2,1,0:T(8,128)(2,1)} %param.12) | copy-start | bytes 1474564
  7.2 122.0 %all-gather.3.cloned.1.call-start = ((), (), s32[]{:S(2)}) async-start(), calls=%async_computation.4 | async-start | bytes 8355840 | tf_op jit(solution)/shard_map/all_gather | solution.py:129
  9.2 10.2 %collective-permute-start = (bf16[160,640]{1,0:T(8,128)(2,1)S(1)}, bf16[160,640]{1,0:T(8,128)(2,1)S(1)}, u32[]{:S(2)}, u32[]{:S(2)}) collective-permute-start(bf16[160,640]{1,0:T(8,128)(2,1)S(1)} %pad_maximum_fusion.2), channel_id=1, source_target_pairs={{0,256},{256,0},{1,257},{257,1},{2,258},{258,2},{3,259},{259,3},{4... | collective-permute-start | bytes 614408 | tf_op jit(solution)/shard_map/ppermute | solution.py:118
  23.3 0.8 copy-start.3
  24.1 12.6 %copy-start.8 = (f32[1,2,16]{2,1,0:T(2,128)S(1)}, f32[1,2,16]{2,1,0:T(2,128)}, u32[]{:S(2)}) copy-start(f32[1,2,16]{2,1,0:T(2,128)} %param.11) | copy-start | bytes 388
  28.4 21.3 %all-to-all-start = ((bf16[16,2,3,8,640]{4,3,2,1,0:T(8,128)(2,1)}), bf16[16,2,3,8,640]{4,3,2,1,0:T(8,128)(2,1)S(1)}, u32[]{:S(2)}, u32[]{:S(2)}) async-start(bf16[16,2,3,8,640]{4,3,2,1,0:T(8,128)(2,1)} %copy_bitcast_fusion), calls=%async_computation | async-start | bytes 1966080 | tf_op jit(solution)/shard_map/all_to_all | solution.py:140
  36.6 188.2 %reduce-scatter.2.cloned.1.call-start = ((), (), s32[]{:S(2)}) async-start(), calls=%async_computation.3 | async-start | bytes 4177920 | tf_op jit(solution)/shard_map/reduce_scatter | solution.py:152
  129.2 3.2 %copy-start.2 = (bf16[6144,640]{1,0:T(8,128)(2,1)S(1)}, bf16[6144,640]{1,0:T(8,128)(2,1)}, u32[]{:S(2)}) copy-start(bf16[6144,640]{1,0:T(8,128)(2,1)} %all-gather.3.cloned.1.call-done) | copy-start | bytes 23592964
  145.3 2.0 copy-start.1
  147.3 1.2 copy-start.9
  148.5 20.7 %copy-start.6 = (bf16[3,128,640]{2,1,0:T(8,128)(2,1)S(1)}, bf16[3,128,640]{2,1,0:T(8,128)(2,1)}, u32[]{:S(2)}) copy-start(bf16[3,128,640]{2,1,0:T(8,128)(2,1)} %param.12) | copy-start | bytes 1474564
  149.2 20.4 %copy-start.7 = (f32[3,128,128]{2,1,0:T(8,128)S(1)}, f32[3,128,128]{2,1,0:T(8,128)}, u32[]{:S(2)}) copy-start(f32[3,128,128]{2,1,0:T(8,128)} %get-tuple-element.25) | copy-start | bytes 589828
  150.3 18.9 %all-to-all-start.1 = ((bf16[16,2,3,8,640]{4,3,2,1,0:T(8,128)(2,1)}), bf16[16,2,3,8,640]{4,3,2,1,0:T(8,128)(2,1)S(1)}, u32[]{:S(2)}, u32[]{:S(2)}) async-start(bf16[16,2,3,8,640]{4,3,2,1,0:T(8,128)(2,1)} %pad_maximum_fusion.1), calls=%async_computation.1 | async-start | bytes 1966080 | tf_op jit(solution)/shard_map/all_to_all | solution.py:161
  225.9 8.3 %collective-permute-start.1 = (bf16[20,2560]{1,0:T(8,128)(2,1)S(1)}, bf16[20,2560]{1,0:T(8,128)(2,1)S(1)}, u32[]{:S(2)}, u32[]{:S(2)}) collective-permute-start(bf16[20,2560]{1,0:T(8,128)(2,1)S(1)} %broadcast_select_fusion.2), channel_id=1, source_target_pairs={{0,256},{256,0},{1,257},{257,1},{2,258},{258,2},{3,259},{259,3},{4... | collective-permute-start | bytes 307208 | tf_op jit(solution)/shard_map/ppermute | solution.py:155
Sparse Core Ops, SparseCore 0:
  24.2 105.0 all-gather.2
  147.5 77.3 reduce-scatter.1

commit v2 on v1

v2 whole, which is shorter than its diff:
```python
import jax
import jax.numpy as jnp
import numpy as np
from jax import lax
from jax.experimental import pallas as pl
from jax.experimental.pallas import tpu as pltpu
from jax.sharding import Mesh
from jax.sharding import PartitionSpec as P

PAD = 48
CHUNK = 640
STRIDE = 64
SWAP = ((0, 1), (1, 0))
C0 = 0.7978845608028654
C1 = 0.044715


def hidden_kernel(scale_ref, rows_ref, grad_ref, w_in_ref, w_out_ref, dw_ref, hidden_ref, dpre_ref):
    scale_in = scale_ref[0]
    scale_out = scale_ref[1]
    rows = rows_ref[...]
    grad = grad_ref[...]
    w_in = w_in_ref[...].reshape(rows.shape[1], -1)
    w_out = w_out_ref[...].reshape(-1, grad.shape[1])
    pre = jnp.dot(rows, w_in, preferred_element_type=jnp.float32) * scale_in
    d_hidden = (
        lax.dot_general(grad, w_out, (((1,), (1,)), ((), ())), preferred_element_type=jnp.float32)
        * scale_out
    )
    square = pre * pre
    tanh = jnp.tanh(C0 * (pre + C1 * (square * pre)))
    half = 0.5 * (1.0 + tanh)
    hidden_ref[...] = (pre * half).astype(jnp.bfloat16)
    slope = half + (0.5 * C0) * pre * (1.0 - tanh * tanh) * (1.0 + (3.0 * C1) * square)
    d_pre = (slope * d_hidden).astype(jnp.bfloat16)
    dpre_ref[...] = d_pre
    dw = lax.dot_general(rows, d_pre, (((0,), (0,)), ((), ())), preferred_element_type=jnp.float32)
    dw = (dw * scale_in).astype(dw_ref.dtype)
    for z in range(dw.shape[0] // PAD):
        dw_ref[z * STRIDE : z * STRIDE + PAD] = dw[z * PAD : (z + 1) * PAD]
        dw_ref[z * STRIDE + PAD : (z + 1) * STRIDE] = jnp.zeros((STRIDE - PAD, CHUNK), dw_ref.dtype)


def hidden_of(scales, rows, grads, weights):
    count, depth = rows.shape
    width = grads.shape[1]
    zs = weights.shape[0]
    chunks = 2
    by_chunk = pl.BlockSpec((count, CHUNK), lambda r: (0, r))
    return pl.pallas_call(
        hidden_kernel,
        grid=(chunks,),
        in_specs=[
            pl.BlockSpec(memory_space=pltpu.SMEM),
            pl.BlockSpec((count, depth), lambda r: (0, 0)),
            pl.BlockSpec((count, width), lambda r: (0, 0)),
            pl.BlockSpec((zs, PAD, CHUNK), lambda r: (0, 2 + r, 0)),
            pl.BlockSpec((zs // 2, 80, width), lambda r: (r, 0, 0)),
        ],
        out_specs=[pl.BlockSpec((zs * STRIDE, CHUNK), lambda r: (0, r)), by_chunk, by_chunk],
        out_shape=[
            jax.ShapeDtypeStruct((zs * STRIDE, chunks * CHUNK), jnp.bfloat16),
            jax.ShapeDtypeStruct((count, chunks * CHUNK), jnp.bfloat16),
            jax.ShapeDtypeStruct((count, chunks * CHUNK), jnp.bfloat16),
        ],
        compiler_params=pltpu.CompilerParams(vmem_limit_bytes=40 * 1024 * 1024),
        cost_estimate=pl.CostEstimate(
            flops=6 * count * width * chunks * CHUNK,
            bytes_accessed=16 * 1024 * 1024,
            transcendentals=count * chunks * CHUNK,
        ),
    )(scales, rows, grads, weights, weights)


def rows_kernel(
    scale_ref, hidden_ref, dpre_ref, w_in_ref, w_out_ref,
    out_own_ref, drow_own_ref, out_sent_ref, drow_sent_ref, peak_ref, out_acc, drow_acc,
):
    step = pl.program_id(0)
    scale_in = scale_ref[0]
    scale_out = scale_ref[1]
    w_in = w_in_ref[...].reshape(drow_acc.shape[1], -1)
    w_out = w_out_ref[...].reshape(-1, out_acc.shape[1])
    out = jnp.dot(hidden_ref[...], w_out, preferred_element_type=jnp.float32)
    drow = lax.dot_general(
        dpre_ref[...], w_in, (((1,), (1,)), ((), ())), preferred_element_type=jnp.float32
    )
    peak_in = jnp.max(jnp.abs(w_in.astype(jnp.float32)), axis=0, keepdims=True)
    peak_out = jnp.max(jnp.abs(w_out.astype(jnp.float32)), axis=0, keepdims=True)

    @pl.when(step == 0)
    def _():
        out_acc[...] = out
        drow_acc[...] = drow
        peak_ref[:, :CHUNK] = jnp.broadcast_to(peak_in, (8, CHUNK))
        peak_ref[:, CHUNK:] = jnp.broadcast_to(peak_out, (8, CHUNK))

    @pl.when(step > 0)
    def _():
        count = out_own_ref.shape[0]
        width = out_own_ref.shape[1]
        out_sum = (out_acc[...] + out) * scale_out
        drow_sum = (drow_acc[...] + drow) * scale_in
        out_own_ref[...] = out_sum[:count]
        drow_own_ref[...] = drow_sum[:count]
        out_sent_ref[...] = out_sum[count:].astype(out_sent_ref.dtype)
        drow_sent_ref[...] = drow_sum[count:].astype(drow_sent_ref.dtype)
        peak_ref[:, :CHUNK] = jnp.maximum(peak_ref[:, :CHUNK], peak_in)
        peak_ref[:, CHUNK:] = jnp.maximum(peak_ref[:, CHUNK:], peak_out)


def rows_of(scales, hidden, dpre, weights, depth):
    count = hidden.shape[0]
    zs, _, width = weights.shape
    chunks = 2
    half = count // 2
    by_chunk = pl.BlockSpec((count, CHUNK), lambda r: (0, r))
    return pl.pallas_call(
        rows_kernel,
        grid=(chunks,),
        in_specs=[
            pl.BlockSpec(memory_space=pltpu.SMEM),
            by_chunk,
            by_chunk,
            pl.BlockSpec((zs, PAD, CHUNK), lambda r: (0, 2 + r, 0)),
            pl.BlockSpec((zs // 2, 80, width), lambda r: (r, 0, 0)),
        ],
        out_specs=[
            pl.BlockSpec((half, width), lambda r: (0, 0)),
            pl.BlockSpec((half, depth), lambda r: (0, 0)),
            pl.BlockSpec((half, width), lambda r: (0, 0)),
            pl.BlockSpec((half, depth), lambda r: (0, 0)),
            pl.BlockSpec((8, 2 * CHUNK), lambda r: (0, 0)),
        ],
        out_shape=[
            jax.ShapeDtypeStruct((half, width), jnp.float32),
            jax.ShapeDtypeStruct((half, depth), jnp.float32),
            jax.ShapeDtypeStruct((half, width), jnp.bfloat16),
            jax.ShapeDtypeStruct((half, depth), jnp.bfloat16),
            jax.ShapeDtypeStruct((8, 2 * CHUNK), jnp.float32),
        ],
        scratch_shapes=[
            pltpu.VMEM((count, width), jnp.float32),
            pltpu.VMEM((count, depth), jnp.float32),
        ],
        compiler_params=pltpu.CompilerParams(vmem_limit_bytes=40 * 1024 * 1024),
        cost_estimate=pl.CostEstimate(
            flops=4 * count * width * chunks * CHUNK,
            bytes_accessed=16 * 1024 * 1024,
            transcendentals=0,
        ),
    )(scales, hidden, dpre, weights, weights)


def placement(width, zs):
    per = width // (2 * zs)
    table = np.zeros((width, zs * PAD), np.float32)
    for half in range(2):
        for z in range(zs):
            for i in range(per):
                table[(half * zs + z) * per + i, z * PAD + half * per + i] = 1.0
    return table


def body(images, router, w_in, w_out, history, cotangent):
    bf16 = jnp.bfloat16
    f32 = jnp.float32
    width = images.shape[2]
    count = images.shape[0]
    zs = lax.axis_size("z")
    n_expert = lax.axis_size("x") * lax.axis_size("yl") * lax.axis_size("c")
    per_expert = router.shape[1] // n_expert
    along = ("x", "yl", "c")
    yh = lax.axis_index("yh")

    local = w_in[0]
    ff = local.shape[1] // 2
    stay = jnp.where(yh == 0, local[:, :ff], local[:, ff:])
    swap = jnp.where(yh == 0, local[:, ff:], local[:, :ff])
    got = lax.ppermute(swap, "yh", SWAP)
    stay = jnp.stack([stay[:, :CHUNK], stay[:, CHUNK:]])
    got = jnp.stack([got[:, :CHUNK], got[:, CHUNK:]])
    low = jnp.where(yh == 0, stay, got)
    high = jnp.where(yh == 0, got, stay)
    gap = jnp.zeros((2, PAD - 40, CHUNK), bf16)
    in_part = jnp.concatenate([low, high, gap], 1).reshape(2 * PAD, CHUNK)
    block = jnp.concatenate([w_out[0], jnp.zeros((16, CHUNK), bf16), in_part], 0)
    weights = lax.all_gather(block, "z", axis=0, tiled=False)

    scales = jnp.max(history[0], axis=1) / 448.0

    logits = jnp.einsum("bpd,ds->bps", images, router, preferred_element_type=f32)
    dispatch = jax.nn.softmax(logits, axis=1)
    combine = jax.nn.softmax(logits, axis=2)
    dispatch_b = dispatch.astype(bf16)
    combine_b = combine.astype(bf16)
    slot_in = jnp.einsum("bps,bpd->bsd", dispatch_b, images, preferred_element_type=f32).astype(bf16)
    d_slot_out = jnp.einsum("bps,bpd->bsd", combine_b, cotangent, preferred_element_type=f32).astype(bf16)
    both = jnp.stack([slot_in, d_slot_out]).reshape(2, count, n_expert, per_expert, width)
    both = both.transpose(2, 0, 1, 3, 4)
    routed = lax.all_to_all(both, along, split_axis=0, concat_axis=0, tiled=True)
    routed = routed.transpose(1, 0, 2, 3, 4).reshape(2, -1, width)
    twin = lax.ppermute(routed, "yh", SWAP)
    rows = jnp.concatenate([routed[0], twin[0]], 0)
    grads = jnp.concatenate([routed[1], twin[1]], 0)
    spread = jnp.asarray(placement(width, zs), bf16)
    rows = jnp.dot(rows, spread, preferred_element_type=f32).astype(bf16)

    dw, hidden, dpre = hidden_of(scales, rows, grads, weights)

    out_own, drow_own, out_sent, drow_sent, peaks = rows_of(scales, hidden, dpre, weights, rows.shape[1])
    fetched = lax.ppermute(jnp.concatenate([out_sent, drow_sent], 1), "yh", SWAP)
    rows_out = (out_own + fetched[:, :width].astype(f32)).astype(bf16)
    d_rows = (drow_own + fetched[:, width:].astype(f32)).astype(bf16)
    d_rows = lax.dot_general(
        d_rows, spread, (((1,), (1,)), ((), ())), preferred_element_type=f32
    ).astype(bf16)
    back = jnp.stack(
        [rows_out.reshape(n_expert, -1, width), d_rows.reshape(n_expert, -1, width)], 1
    ).reshape(n_expert, 2, count, per_expert, width)
    returned = lax.all_to_all(back, along, split_axis=0, concat_axis=0, tiled=True)
    returned = returned.transpose(1, 2, 0, 3, 4).reshape(2, count, -1, width)

    part = lax.psum_scatter(dw, "z", scatter_dimension=0, tiled=True)
    keep = jnp.where(yh == 0, part[:20], part[20:40])
    give = jnp.where(yh == 0, part[20:40], part[:20])
    peaks = peaks[:1].astype(bf16)
    got = lax.ppermute(jnp.concatenate([give, peaks], 0), "yh", SWAP)
    theirs = got[:20]
    d_w_in = jnp.concatenate(
        [jnp.where(yh == 0, keep, theirs), jnp.where(yh == 0, theirs, keep)], 1
    )[None]
    peaks = jnp.maximum(peaks[0], got[20]).reshape(2, -1).astype(f32)
    peaks = jnp.max(peaks, axis=1, keepdims=True)
    new_history = jnp.concatenate([peaks, history[0, :, :-1]], axis=1)[None]

    slot_out = returned[0]
    d_slot_in = returned[1]
    output = jnp.einsum("bps,bsd->bpd", combine_b, slot_out, preferred_element_type=f32).astype(bf16)
    d_combine = jnp.einsum("bpd,bsd->bps", cotangent, slot_out, preferred_element_type=f32)
    d_dispatch = jnp.einsum("bpd,bsd->bps", images, d_slot_in, preferred_element_type=f32)
    d_logits = dispatch * (d_dispatch - jnp.sum(dispatch * d_dispatch, axis=1, keepdims=True))
    d_logits = d_logits + combine * (d_combine - jnp.sum(combine * d_combine, axis=2, keepdims=True))
    d_logits = d_logits.astype(bf16)
    d_images = jnp.einsum("bps,bsd->bpd", dispatch_b, d_slot_in, preferred_element_type=f32)
    d_images = d_images + jnp.einsum("bps,ds->bpd", d_logits, router, preferred_element_type=f32)
    d_images = d_images.astype(bf16)
    return (output, d_images, d_w_in, new_history)


def solution(mesh):
    fine = Mesh(mesh.devices.reshape(2, 16, 4, 2, 2), ("yh", "z", "x", "yl", "c"))
    dp = ("yh", "z")
    expert = ("x", "yl", "c")
    every = dp + expert
    return jax.shard_map(
        body,
        mesh=fine,
        in_specs=(
            P(every, None, None),
            P(),
            P(expert, dp, None),
            P(expert, dp, None),
            P(expert, None, None),
            P(every, None, None),
        ),
        out_specs=(
            P(every, None, None),
            P(every, None, None),
            P(expert, dp, None),
            P(expert, None, None),
        ),
        check_vma=False,
    )
```

time: 243 us -> 202 us (0.83)
  the two profiles are of different devices: /device:TPU:12 before, /device:TPU:2 now
where the time goes in v2:
time: 202 us
  waiting for transfers between devices  95.7 us (47%)
  starting transfers between devices  23.4 us (12%)
  blocking collectives  21.7 us (11%)
  between operations  14.4 us (7%)
  Pallas kernels  13.7 us (7%)
  local copies, waits for them, and re-layouts  11.6 us (6%)
  matrix products  11.1 us (5%)
  other arithmetic  10 us (5%)
    all_gather x1, waiting for transfers between devices, body(): weights = lax.all_gather(block, 'z', axis=0, tiled=False)  25.4 us
    ppermute x1, waiting for transfers between devices, body(): twin = lax.ppermute(routed, 'yh', SWAP)  25 us
    all_to_all x1, blocking collectives, body(): lax.all_to_all(both, along, split_axis=0, concat_axis=0, tiled=True)  21.7 us
    ppermute x1, waiting for transfers between devices, body(): lax.ppermute(jnp.concatenate([out_sent, drow_sent], 1), 'yh', SWAP)  15.9 us
    all_to_all x1, waiting for transfers between devices, body(): lax.all_to_all(back, along, split_axis=0, concat_axis=0, tiled=True)  13.6 us
    reduce_scatter x1, waiting for transfers between devices, body(): part = lax.psum_scatter(dw, 'z', scatter_dimension=0, tiled=True)  13.3 us
    unnamed x32, local copies, waits for them, and re-layouts  10 us
    pallas_call x1, Pallas kernels, hidden_of(): pl.pallas_call(hidden_kernel, grid=(chunks,), in_specs=[pl.BlockSpec(memo...  8.06 us
  transfers between devices with their start and end apart: 7, of which 6 were waited for; matrix products, arithmetic and copies ran while one was open for 9% of the time, Pallas kernels for 3%

profile of v2, /device:TPU:2, one launch (start us, length us, event | category | flops | bytes accessed | tf_op | source)
XLA Modules:
  0.0 201.6 jit_solution(8317901793687202388)
XLA Ops:
  7.2 0.9 broadcast_select_fusion.5
  8.2 5.1 %collective-permute-start.1 = (bf16[20,1280]{1,0:T(8,128)(2,1)S(1)}, bf16[20,1280]{1,0:T(8,128)(2,1)S(1)}, u32[]{:S(2)}, u32[]{:S(2)}) collective-permute-start(bf16[20,1280]{1,0:T(8,128)(2,1)S(1)} %get-tuple-element.31), channel_id=1, source_target_pairs={{0,256},{256,0},{1,257},{257,1},{2,258},{258,2},{3,259},{259,3},{4... | collective-permute-start | bytes 153608 | tf_op jit(solution)/shard_map/ppermute | solution.py:180
  13.5 2.3 %collective-permute-done.1 = bf16[20,1280]{1,0:T(8,128)(2,1)S(1)} collective-permute-done((bf16[20,1280]{1,0:T(8,128)(2,1)S(1)}, bf16[20,1280]{1,0:T(8,128)(2,1)S(1)}, u32[]{:S(2)}, u32[]{:S(2)}) %collective-permute-start.1) | collective-permute-done | bytes 51232 | tf_op jit(solution)/shard_map/ppermute | solution.py:180
  15.9 1.7 pad_maximum_fusion.4
  19.2 0.8 fusion.45
  20.0 0.9 fusion.6
  21.0 21.7 %all_to_all.10 = bf16[16,2,3,8,640]{4,3,2,1,0:T(8,128)(2,1)S(1)} all-to-all(bf16[16,2,3,8,640]{4,3,2,1,0:T(8,128)(2,1)S(1)} %copy_bitcast_fusion), channel_id=1, replica_groups=mesh['yh'=2,'z'=16,'x'=4,'yl'=2,'c'=2] {'x','yl','c'}, dimensions={0} | all-to-all | bytes 1966080 | tf_op jit(solution)/shard_map/all_to_all | solution.py:201
  42.8 1.0 copy.23
  43.8 2.1 %collective-permute-start = (bf16[2,384,640]{2,1,0:T(8,128)(2,1)}, bf16[2,384,640]{2,1,0:T(8,128)(2,1)S(1)}, u32[]{:S(2)}, u32[]{:S(2)}) collective-permute-start(bf16[2,384,640]{2,1,0:T(8,128)(2,1)} %bitcast.6), channel_id=1, source_target_pairs={{0,256},{256,0},{1,257},{257,1},{2,258},{258,2},{3,259},{259,3},{4... | collective-permute-start | bytes 2949128 | tf_op jit(solution)/shard_map/ppermute | solution.py:203
  46.2 25.0 %collective-permute-done = bf16[2,384,640]{2,1,0:T(8,128)(2,1)S(1)} collective-permute-done((bf16[2,384,640]{2,1,0:T(8,128)(2,1)}, bf16[2,384,640]{2,1,0:T(8,128)(2,1)S(1)}, u32[]{:S(2)}, u32[]{:S(2)}) %collective-permute-start) | collective-permute-done | bytes 983072 | tf_op jit(solution)/shard_map/ppermute | solution.py:203
  71.4 1.1 copy-done.7
  72.5 2.1 %convolution_convert_fusion.rows_ref = bf16[768,768]{1,0:T(8,128)(2,1)} fusion(bf16[640,768]{1,0:T(8,128)(2,1)S(1)} %copy-done.7, bf16[384,640]{1,0:T(8,128)(2,1)S(1)} %get-tuple-element.25, bf16[384,640]{1,0:T(8,128)(2,1)S(1)} %bitcast.85), kind=kOutput, calls=%fused_computation.4 | convolution fusion | flops 757530624 | bytes 3145728 | tf_op jit(solution)/shard_map/dot_general | solution.py:207
  74.6 25.4 %all-gather.3.cloned.1.call-done = bf16[3072,640]{1,0:T(8,128)(2,1)} async-done(((bf16[192,640]{1,0:T(8,128)(2,1)}), bf16[3072,640]{1,0:T(8,128)(2,1)}) %all-gather.3.cloned.1.call-update) | async-done | bytes 3932176 | tf_op jit(solution)/shard_map/all_gather | solution.py:188
  100.1 2.1 %copy-done.1 = bf16[3072,640]{1,0:T(8,128)(2,1)S(1)} copy-done((bf16[3072,640]{1,0:T(8,128)(2,1)S(1)}, bf16[3072,640]{1,0:T(8,128)(2,1)}, u32[]{:S(2)}) %copy-start.1) | copy-done | bytes 3932184
  102.2 1.3 copy-done.5
  103.4 8.1 %shard_map.102 = (bf16[1024,1280]{1,0:T(8,128)(2,1)}, bf16[768,1280]{1,0:T(8,128)(2,1)S(1)}, bf16[768,1280]{1,0:T(8,128)(2,1)S(1)}) custom-call(f32[2]{0:T(128)S(1)} %broadcast_multiply_fusion.scale_ref, bf16[768,768]{1,0:T(8,128)(2,1)S(1)} %copy-done.5, bf16[768,640]{1,0:T(8,128)(2,1)S(1)} %pad_maximum_fusion.2.grad_ref, ...), custom_call_target="tpu_custom_call" | custom-call | flops 3774873600 | bytes 16777216 | tf_op jit(solution)/shard_map/pallas_call | solution.py:50
  111.5 1.3 copy-done.3
  112.8 2.1 %copy-done.2 = bf16[3072,640]{1,0:T(8,128)(2,1)S(1)} copy-done((bf16[3072,640]{1,0:T(8,128)(2,1)S(1)}, bf16[3072,640]{1,0:T(8,128)(2,1)}, u32[]{:S(2)}) %copy-start.2) | copy-done | bytes 3932184
  115.0 1.5 copy-done.4
  116.5 5.6 %shard_map.103 = (f32[384,640]{1,0:T(8,128)S(1)}, f32[384,768]{1,0:T(8,128)S(1)}, bf16[384,640]{1,0:T(8,128)(2,1)S(1)}, bf16[384,768]{1,0:T(8,128)(2,1)S(1)}, f32[8,1280]{1,0:T(8,128)S(1)}) custom-call(f32[2]{0:T(128)S(1)} %broadcast_multiply_fusion.scale_ref, bf16[768,1280]{1,0:T(8,128)(2,1)S(1)} %get-tuple-element.12.hidden_ref, ...), custom_call_target="tpu_custom_call" | custom-call | flops 2516582400 | bytes 16777216 | tf_op jit(solution)/shard_map/pallas_call | solution.py:118
  122.2 5.0 %collective-permute-start.2 = (bf16[384,1408]{1,0:T(8,128)(2,1)S(1)}, bf16[384,1408]{1,0:T(8,128)(2,1)S(1)}, u32[]{:S(2)}, u32[]{:S(2)}) collective-permute-start(bf16[384,1408]{1,0:T(8,128)(2,1)S(1)} %pad_maximum_fusion), channel_id=1, source_target_pairs={{0,256},{256,0},{1,257},{257,1},{2,258},{258,2},{3,259},{259,3},{4... | collective-permute-start | bytes 3244040 | tf_op jit(solution)/shard_map/ppermute | solution.py:212
  127.3 15.9 %collective-permute-done.2 = bf16[384,1408]{1,0:T(8,128)(2,1)S(1)} collective-permute-done((bf16[384,1408]{1,0:T(8,128)(2,1)S(1)}, bf16[384,1408]{1,0:T(8,128)(2,1)S(1)}, u32[]{:S(2)}, u32[]{:S(2)}) %collective-permute-start.2) | collective-permute-done | bytes 1081376 | tf_op jit(solution)/shard_map/ppermute | solution.py:212
  144.0 1.1 pad_maximum_fusion.3
  145.1 5.7 %all-to-all-start.1 = ((bf16[16,2,3,8,640]{4,3,2,1,0:T(8,128)(2,1)}), bf16[16,2,3,8,640]{4,3,2,1,0:T(8,128)(2,1)S(1)}, u32[]{:S(2)}, u32[]{:S(2)}) async-start(bf16[16,2,3,8,640]{4,3,2,1,0:T(8,128)(2,1)} %pad_maximum_fusion.3), calls=%async_computation.1 | async-start | bytes 1966080 | tf_op jit(solution)/shard_map/all_to_all | solution.py:221
  150.8 13.6 %all-to-all-done.1 = bf16[16,2,3,8,640]{4,3,2,1,0:T(8,128)(2,1)S(1)} async-done(((bf16[16,2,3,8,640]{4,3,2,1,0:T(8,128)(2,1)}), bf16[16,2,3,8,640]{4,3,2,1,0:T(8,128)(2,1)S(1)}, u32[]{:S(2)}, u32[]{:S(2)}) %all-to-all-start.1) | async-done | bytes 983072 | tf_op jit(solution)/shard_map/all_to_all | solution.py:221
  165.3 1.6 fusion.13
  167.3 1.3 fusion.22
  168.6 2.1 %fusion.4 = bf16[3,128,640]{2,1,0:T(8,128)(2,1)} fusion(f32[3,128,640]{2,1,0:T(8,128)S(1)} %fusion.22, f32[3,128,128]{2,1,0:T(8,128)S(1)} %fusion.13, f32[3,128,128]{2,1,0:T(8,128)S(1)} %convolution_bitcast_fusion.1, bf16[640,128]{1,0:T(8,128)(2,1)S(1)} %copy-done.10, f32[3,128,128]{2,1,0:T(8,128)} %get-tuple-element.39, f32[3,128]{1,0:T(4,128)S(1)} %get-tuple-element.38), kind=kOutput, calls=%fused_computation.6 | convolution fusion | flops 63750656 | bytes 2229760 | tf_op jit(solution)/shard_map/bps,ds->bpd/dot_general | solution.py:246
  170.8 13.3 %reduce-scatter.2.cloned.1.call-done = bf16[64,1280]{1,0:T(8,128)(2,1)} async-done(((bf16[1024,1280]{1,0:T(8,128)(2,1)}), bf16[64,1280]{1,0:T(8,128)(2,1)}) %reduce-scatter.2.cloned.1.call-update) | async-done | bytes 163856 | tf_op jit(solution)/shard_map/reduce_scatter | solution.py:224
  184.1 1.0 broadcast_select_fusion.2
  185.1 5.4 %collective-permute-start.3 = (bf16[21,1280]{1,0:T(8,128)(2,1)S(1)}, bf16[21,1280]{1,0:T(8,128)(2,1)S(1)}, u32[]{:S(2)}, u32[]{:S(2)}) collective-permute-start(bf16[21,1280]{1,0:T(8,128)(2,1)S(1)} %pad_maximum_fusion.7), channel_id=1, source_target_pairs={{0,256},{256,0},{1,257},{257,1},{2,258},{258,2},{3,259},{259,3},{4... | collective-permute-start | bytes 161288 | tf_op jit(solution)/shard_map/ppermute | solution.py:228
  190.5 2.6 %convolution_convert_fusion.1 = bf16[3,128,640]{2,1,0:T(8,128)(2,1)} fusion(bf16[1,3,16,8,640]{4,3,1,0,2:T(8,128)(2,1)S(1)} %get-tuple-element.21, f32[3,128]{1,0:T(4,128)S(1)} %get-tuple-element.36, f32[3,128,128]{2,1,0:T(8,128)} %copy-done.6), kind=kOutput, calls=%fused_computation.7 | convolution fusion | flops 63308288 | bytes 1181184 | tf_op jit(solution)/shard_map/bps,bsd->bpd/dot_general | solution.py:239
  (65 shorter events, 6.1 us)
Async XLA Ops:
  7.2 10.5 %copy-start = (bf16[3,128,640]{2,1,0:T(8,128)(2,1)S(1)}, bf16[3,128,640]{2,1,0:T(8,128)(2,1)}, u32[]{:S(2)}) copy-start(bf16[3,128,640]{2,1,0:T(8,128)(2,1)} %param.7) | copy-start | bytes 1474564
  7.2 10.5 %copy-start.9 = (bf16[640,128]{1,0:T(8,128)(2,1)S(1)}, bf16[640,128]{1,0:T(8,128)(2,1)}, u32[]{:S(2)}) copy-start(bf16[640,128]{1,0:T(8,128)(2,1)} %param.8) | copy-start | bytes 491524
  7.2 92.9 %all-gather.3.cloned.1.call-start = ((), (), s32[]{:S(2)}) async-start(), calls=%async_computation.4 | async-start | bytes 4177920 | tf_op jit(solution)/shard_map/all_gather | solution.py:188
  8.2 7.6 %collective-permute-start.1 = (bf16[20,1280]{1,0:T(8,128)(2,1)S(1)}, bf16[20,1280]{1,0:T(8,128)(2,1)S(1)}, u32[]{:S(2)}, u32[]{:S(2)}) collective-permute-start(bf16[20,1280]{1,0:T(8,128)(2,1)S(1)} %get-tuple-element.31), channel_id=1, source_target_pairs={{0,256},{256,0},{1,257},{257,1},{2,258},{258,2},{3,259},{259,3},{4... | collective-permute-start | bytes 153608 | tf_op jit(solution)/shard_map/ppermute | solution.py:180
  17.6 2.4 %copy-start.11 = (bf16[3,128,640]{2,1,0:T(8,128)(2,1)S(1)}, bf16[3,128,640]{2,1,0:T(8,128)(2,1)}, u32[]{:S(2)}) copy-start(bf16[3,128,640]{2,1,0:T(8,128)(2,1)} %param.12) | copy-start | bytes 1474564
  17.7 166.4 %reduce-scatter.2.cloned.1.call-start = ((), (), s32[]{:S(2)}) async-start(), calls=%async_computation.3 | async-start | bytes 2785280 | tf_op jit(solution)/shard_map/reduce_scatter | solution.py:224
  18.0 2.9 %copy-start.6 = (f32[3,128,128]{2,1,0:T(8,128)}, f32[3,128,128]{2,1,0:T(8,128)S(1)}, u32[]{:S(2)}) copy-start(f32[3,128,128]{2,1,0:T(8,128)S(1)} %fusion.34) | copy-start | bytes 589828
  42.8 3.2 %copy-start.15 = (f32[1,2,16]{2,1,0:T(2,128)S(1)}, f32[1,2,16]{2,1,0:T(2,128)}, u32[]{:S(2)}) copy-start(f32[1,2,16]{2,1,0:T(2,128)} %param.11) | copy-start | bytes 388
  43.8 27.4 %collective-permute-start = (bf16[2,384,640]{2,1,0:T(8,128)(2,1)}, bf16[2,384,640]{2,1,0:T(8,128)(2,1)S(1)}, u32[]{:S(2)}, u32[]{:S(2)}) collective-permute-start(bf16[2,384,640]{2,1,0:T(8,128)(2,1)} %bitcast.6), channel_id=1, source_target_pairs={{0,256},{256,0},{1,257},{257,1},{2,258},{258,2},{3,259},{259,3},{4... | collective-permute-start | bytes 2949128 | tf_op jit(solution)/shard_map/ppermute | solution.py:203
  71.3 1.2 copy-start.7
  100.1 2.1 %copy-start.1 = (bf16[3072,640]{1,0:T(8,128)(2,1)S(1)}, bf16[3072,640]{1,0:T(8,128)(2,1)}, u32[]{:S(2)}) copy-start(bf16[3072,640]{1,0:T(8,128)(2,1)} %all-gather.3.cloned.1.call-done) | copy-start | bytes 11796484
  102.2 1.3 copy-start.5
  111.5 1.3 copy-start.3
  112.8 2.1 %copy-start.2 = (bf16[3072,640]{1,0:T(8,128)(2,1)S(1)}, bf16[3072,640]{1,0:T(8,128)(2,1)}, u32[]{:S(2)}) copy-start(bf16[3072,640]{1,0:T(8,128)(2,1)} %all-gather.3.cloned.1.call-done) | copy-start | bytes 11796484
  115.0 1.5 copy-start.4
  122.2 21.1 %copy-start.8 = (bf16[640,768]{1,0:T(8,128)(2,1)S(1)}, bf16[640,768]{1,0:T(8,128)(2,1)}, u32[]{:S(2)}) copy-start(bf16[640,768]{1,0:T(8,128)(2,1)} %constant.23.clone) | copy-start | bytes 2949124
  122.2 21.0 %collective-permute-start.2 = (bf16[384,1408]{1,0:T(8,128)(2,1)S(1)}, bf16[384,1408]{1,0:T(8,128)(2,1)S(1)}, u32[]{:S(2)}, u32[]{:S(2)}) collective-permute-start(bf16[384,1408]{1,0:T(8,128)(2,1)S(1)} %pad_maximum_fusion), channel_id=1, source_target_pairs={{0,256},{256,0},{1,257},{257,1},{2,258},{258,2},{3,259},{259,3},{4... | collective-permute-start | bytes 3244040 | tf_op jit(solution)/shard_map/ppermute | solution.py:212
  145.1 19.3 %all-to-all-start.1 = ((bf16[16,2,3,8,640]{4,3,2,1,0:T(8,128)(2,1)}), bf16[16,2,3,8,640]{4,3,2,1,0:T(8,128)(2,1)S(1)}, u32[]{:S(2)}, u32[]{:S(2)}) async-start(bf16[16,2,3,8,640]{4,3,2,1,0:T(8,128)(2,1)} %pad_maximum_fusion.3), calls=%async_computation.1 | async-start | bytes 1966080 | tf_op jit(solution)/shard_map/all_to_all | solution.py:221
  150.7 13.7 %copy-start.12 = (bf16[3,128,640]{2,1,0:T(8,128)(2,1)S(1)}, bf16[3,128,640]{2,1,0:T(8,128)(2,1)}, u32[]{:S(2)}) copy-start(bf16[3,128,640]{2,1,0:T(8,128)(2,1)} %param.12) | copy-start | bytes 1474564
  164.4 0.9 copy-start.14
  166.9 1.7 copy-start.10
  184.1 10.0 %copy-start.13 = (bf16[64,1280]{1,0:T(8,128)(2,1)S(1)}, bf16[64,1280]{1,0:T(8,128)(2,1)}, u32[]{:S(2)}) copy-start(bf16[64,1280]{1,0:T(8,128)(2,1)} %reduce-scatter.2.cloned.1.call-done) | copy-start | bytes 491524
  185.1 8.0 %collective-permute-start.3 = (bf16[21,1280]{1,0:T(8,128)(2,1)S(1)}, bf16[21,1280]{1,0:T(8,128)(2,1)S(1)}, u32[]{:S(2)}, u32[]{:S(2)}) collective-permute-start(bf16[21,1280]{1,0:T(8,128)(2,1)S(1)} %pad_maximum_fusion.7), channel_id=1, source_target_pairs={{0,256},{256,0},{1,257},{257,1},{2,258},{258,2},{3,259},{259,3},{4... | collective-permute-start | bytes 161288 | tf_op jit(solution)/shard_map/ppermute | solution.py:228
Sparse Core Ops, SparseCore 0:
  17.8 82.2 all-gather.2
  113.0 71.0 reduce-scatter.1

commit v3 on v2

--- a/solution.py
+++ b/solution.py
@@ -63,7 +63,7 @@
             jax.ShapeDtypeStruct((count, chunks * CHUNK), jnp.bfloat16),
             jax.ShapeDtypeStruct((count, chunks * CHUNK), jnp.bfloat16),
         ],
-        compiler_params=pltpu.CompilerParams(vmem_limit_bytes=40 * 1024 * 1024),
+        compiler_params=pltpu.CompilerParams(vmem_limit_bytes=56 * 1024 * 1024),
         cost_estimate=pl.CostEstimate(
             flops=6 * count * width * chunks * CHUNK,
             bytes_accessed=16 * 1024 * 1024,
@@ -143,7 +143,7 @@
             pltpu.VMEM((count, width), jnp.float32),
             pltpu.VMEM((count, depth), jnp.float32),
         ],
-        compiler_params=pltpu.CompilerParams(vmem_limit_bytes=40 * 1024 * 1024),
+        compiler_params=pltpu.CompilerParams(vmem_limit_bytes=56 * 1024 * 1024),
         cost_estimate=pl.CostEstimate(
             flops=4 * count * width * chunks * CHUNK,
             bytes_accessed=16 * 1024 * 1024,

time: 202 us -> 200 us (0.990)
  local copies, waits for them, and re-layouts: 11.6 us -> 3.44 us
  Pallas kernels: 13.7 us -> 17.8 us
  matrix products: 11.1 us -> 8.01 us
  other arithmetic: 10 us -> 13 us
    unnamed x32 -> x20, local copies, waits for them, and re-layouts: 10 us -> 1.06 us
    pallas_call x1, Pallas kernels: 5.6 us -> 8.48 us  [rows_of(): pl.pallas_call(rows_kernel, grid=(chunks,), in_specs=[pl.BlockSpec(memory...]
  transfers between devices with their start and end apart: 7 -> 7, of which waited for: 6 -> 7; matrix products, arithmetic and copies ran while one was open for 9% -> 9% of each run, Pallas kernels for 3% -> 4%
where the time goes in v3:
time: 200 us; the launch traced here: 199 us
  waiting for transfers between devices  97.5 us (49%)
  starting transfers between devices  22.9 us (11%)
  blocking collectives  21.7 us (11%)
  Pallas kernels  17.8 us (9%)
  between operations  14.3 us (7%)
  other arithmetic  13 us (6%)
  matrix products  8.01 us (4%)
  local copies, waits for them, and re-layouts  3.44 us (2%)
    all_gather x1, waiting for transfers between devices, body(): weights = lax.all_gather(block, 'z', axis=0, tiled=False)  25.7 us
    ppermute x1, waiting for transfers between devices, body(): twin = lax.ppermute(routed, 'yh', SWAP)  24.5 us
    all_to_all x1, blocking collectives, body(): lax.all_to_all(both, along, split_axis=0, concat_axis=0, tiled=True)  21.7 us
    ppermute x1, waiting for transfers between devices, body(): lax.ppermute(jnp.concatenate([out_sent, drow_sent], 1), 'yh', SWAP)  16 us
    reduce_scatter x1, waiting for transfers between devices, body(): part = lax.psum_scatter(dw, 'z', scatter_dimension=0, tiled=True)  15 us
    all_to_all x1, waiting for transfers between devices, body(): lax.all_to_all(back, along, split_axis=0, concat_axis=0, tiled=True)  12.9 us
    pallas_call x1, Pallas kernels, hidden_of(): pl.pallas_call(hidden_kernel, grid=(chunks,), in_specs=[pl.BlockSpec(memo...  9.33 us
    pallas_call x1, Pallas kernels, rows_of(): pl.pallas_call(rows_kernel, grid=(chunks,), in_specs=[pl.BlockSpec(memory...  8.48 us
  transfers between devices with their start and end apart: 7, of which 7 were waited for; matrix products, arithmetic and copies ran while one was open for 9% of the time, Pallas kernels for 4%

profile of v3, /device:TPU:2, one launch (start us, length us, event | category | flops | bytes accessed | tf_op | source)
XLA Modules:
  0.0 198.7 jit_solution(9295795752910994176)
XLA Ops:
  7.2 0.9 broadcast_select_fusion.5
  8.2 5.1 %collective-permute-start.1 = (bf16[20,1280]{1,0:T(8,128)(2,1)S(1)}, bf16[20,1280]{1,0:T(8,128)(2,1)S(1)}, u32[]{:S(2)}, u32[]{:S(2)}) collective-permute-start(bf16[20,1280]{1,0:T(8,128)(2,1)S(1)} %get-tuple-element.31), channel_id=1, source_target_pairs={{0,256},{256,0},{1,257},{257,1},{2,258},{258,2},{3,259},{259,3},{4... | collective-permute-start | bytes 153608 | tf_op jit(solution)/shard_map/ppermute | solution.py:180
  13.5 2.3 %collective-permute-done.1 = bf16[20,1280]{1,0:T(8,128)(2,1)S(1)} collective-permute-done((bf16[20,1280]{1,0:T(8,128)(2,1)S(1)}, bf16[20,1280]{1,0:T(8,128)(2,1)S(1)}, u32[]{:S(2)}, u32[]{:S(2)}) %collective-permute-start.1) | collective-permute-done | bytes 51232 | tf_op jit(solution)/shard_map/ppermute | solution.py:180
  15.9 1.7 pad_maximum_fusion.4
  18.6 0.8 fusion.45
  19.4 0.9 fusion.6
  20.4 21.7 %all_to_all.10 = bf16[16,2,3,8,640]{4,3,2,1,0:T(8,128)(2,1)S(1)} all-to-all(bf16[16,2,3,8,640]{4,3,2,1,0:T(8,128)(2,1)S(1)} %copy_bitcast_fusion), channel_id=1, replica_groups=mesh['yh'=2,'z'=16,'x'=4,'yl'=2,'c'=2] {'x','yl','c'}, dimensions={0} | all-to-all | bytes 1966080 | tf_op jit(solution)/shard_map/all_to_all | solution.py:201
  42.2 1.0 copy.23
  43.2 2.1 %collective-permute-start = (bf16[2,384,640]{2,1,0:T(8,128)(2,1)}, bf16[2,384,640]{2,1,0:T(8,128)(2,1)S(1)}, u32[]{:S(2)}, u32[]{:S(2)}) collective-permute-start(bf16[2,384,640]{2,1,0:T(8,128)(2,1)} %bitcast.6), channel_id=1, source_target_pairs={{0,256},{256,0},{1,257},{257,1},{2,258},{258,2},{3,259},{259,3},{4... | collective-permute-start | bytes 2949128 | tf_op jit(solution)/shard_map/ppermute | solution.py:203
  46.1 24.5 %collective-permute-done = bf16[2,384,640]{2,1,0:T(8,128)(2,1)S(1)} collective-permute-done((bf16[2,384,640]{2,1,0:T(8,128)(2,1)}, bf16[2,384,640]{2,1,0:T(8,128)(2,1)S(1)}, u32[]{:S(2)}, u32[]{:S(2)}) %collective-permute-start) | collective-permute-done | bytes 983072 | tf_op jit(solution)/shard_map/ppermute | solution.py:203
  70.7 1.0 pad_maximum_fusion.2.grad_ref
  72.3 2.1 %convolution_convert_fusion.rows_ref = bf16[768,768]{1,0:T(8,128)(2,1)} fusion(bf16[640,768]{1,0:T(8,128)(2,1)S(1)} %copy-done.2, bf16[384,640]{1,0:T(8,128)(2,1)S(1)} %get-tuple-element.25, bf16[384,640]{1,0:T(8,128)(2,1)S(1)} %bitcast.85), kind=kOutput, calls=%fused_computation.4 | convolution fusion | flops 757530624 | bytes 3145728 | tf_op jit(solution)/shard_map/dot_general | solution.py:207
  74.4 25.7 %all-gather.3.cloned.1.call-done = bf16[3072,640]{1,0:T(8,128)(2,1)} async-done(((bf16[192,640]{1,0:T(8,128)(2,1)}), bf16[3072,640]{1,0:T(8,128)(2,1)}) %all-gather.3.cloned.1.call-update) | async-done | bytes 3932176 | tf_op jit(solution)/shard_map/all_gather | solution.py:188
  100.1 9.3 %shard_map.102 = (bf16[1024,1280]{1,0:T(8,128)(2,1)}, bf16[768,1280]{1,0:T(8,128)(2,1)}, bf16[768,1280]{1,0:T(8,128)(2,1)}) custom-call(f32[2]{0:T(128)} %broadcast_multiply_fusion.scale_ref, bf16[768,768]{1,0:T(8,128)(2,1)} %convolution_convert_fusion.rows_ref, bf16[768,640]{1,0:T(8,128)(2,1)} %pad_maximum_fusion.2.grad_ref, ...), custom_call_target="tpu_custom_call" | custom-call | flops 3774873600 | bytes 16777216 | tf_op jit(solution)/shard_map/pallas_call | solution.py:50
  109.4 8.5 %shard_map.103 = (f32[384,640]{1,0:T(8,128)}, f32[384,768]{1,0:T(8,128)}, bf16[384,640]{1,0:T(8,128)(2,1)}, bf16[384,768]{1,0:T(8,128)(2,1)}, f32[8,1280]{1,0:T(8,128)}) custom-call(f32[2]{0:T(128)} %broadcast_multiply_fusion.scale_ref, bf16[768,1280]{1,0:T(8,128)(2,1)} %get-tuple-element.12.hidden_ref, bf16[768,1280]{1,0:T(8,128)(2,1)} %get-tuple-element.13.dpre_ref, ...), custom_call_target="tpu_custom_call" | custom-call | flops 2516582400 | bytes 16777216 | tf_op jit(solution)/shard_map/pallas_call | solution.py:118
  117.9 1.4 pad_maximum_fusion
  119.4 5.0 %collective-permute-start.2 = (bf16[384,1408]{1,0:T(8,128)(2,1)S(1)}, bf16[384,1408]{1,0:T(8,128)(2,1)S(1)}, u32[]{:S(2)}, u32[]{:S(2)}) collective-permute-start(bf16[384,1408]{1,0:T(8,128)(2,1)S(1)} %pad_maximum_fusion), channel_id=1, source_target_pairs={{0,256},{256,0},{1,257},{257,1},{2,258},{258,2},{3,259},{259,3},{4... | collective-permute-start | bytes 3244040 | tf_op jit(solution)/shard_map/ppermute | solution.py:212
  124.3 16.0 %collective-permute-done.2 = bf16[384,1408]{1,0:T(8,128)(2,1)S(1)} collective-permute-done((bf16[384,1408]{1,0:T(8,128)(2,1)S(1)}, bf16[384,1408]{1,0:T(8,128)(2,1)S(1)}, u32[]{:S(2)}, u32[]{:S(2)}) %collective-permute-start.2) | collective-permute-done | bytes 1081376 | tf_op jit(solution)/shard_map/ppermute | solution.py:212
  140.5 0.7 convolution_convert_fusion.2
  141.2 1.1 pad_maximum_fusion.3
  142.2 5.7 %all-to-all-start.1 = ((bf16[16,2,3,8,640]{4,3,2,1,0:T(8,128)(2,1)}), bf16[16,2,3,8,640]{4,3,2,1,0:T(8,128)(2,1)S(1)}, u32[]{:S(2)}, u32[]{:S(2)}) async-start(bf16[16,2,3,8,640]{4,3,2,1,0:T(8,128)(2,1)} %pad_maximum_fusion.3), calls=%async_computation.1 | async-start | bytes 1966080 | tf_op jit(solution)/shard_map/all_to_all | solution.py:221
  147.9 0.8 slice.144
  148.7 12.9 %all-to-all-done.1 = bf16[16,2,3,8,640]{4,3,2,1,0:T(8,128)(2,1)S(1)} async-done(((bf16[16,2,3,8,640]{4,3,2,1,0:T(8,128)(2,1)}), bf16[16,2,3,8,640]{4,3,2,1,0:T(8,128)(2,1)S(1)}, u32[]{:S(2)}, u32[]{:S(2)}) %all-to-all-start.1) | async-done | bytes 983072 | tf_op jit(solution)/shard_map/all_to_all | solution.py:221
  162.4 1.6 fusion.13
  164.7 1.1 fusion.4
  165.8 15.0 %reduce-scatter.2.cloned.1.call-done = bf16[64,1280]{1,0:T(8,128)(2,1)} async-done(((bf16[1024,1280]{1,0:T(8,128)(2,1)}), bf16[64,1280]{1,0:T(8,128)(2,1)}) %reduce-scatter.2.cloned.1.call-update) | async-done | bytes 163856 | tf_op jit(solution)/shard_map/reduce_scatter | solution.py:224
  180.8 1.0 broadcast_select_fusion.2
  181.9 5.0 %collective-permute-start.3 = (bf16[21,1280]{1,0:T(8,128)(2,1)S(1)}, bf16[21,1280]{1,0:T(8,128)(2,1)S(1)}, u32[]{:S(2)}, u32[]{:S(2)}) collective-permute-start(bf16[21,1280]{1,0:T(8,128)(2,1)S(1)} %pad_maximum_fusion.7), channel_id=1, source_target_pairs={{0,256},{256,0},{1,257},{257,1},{2,258},{258,2},{3,259},{259,3},{4... | collective-permute-start | bytes 161288 | tf_op jit(solution)/shard_map/ppermute | solution.py:228
  186.9 1.6 convolution_convert_fusion.1
  188.5 1.0 collective-permute-done.3
  189.5 0.8 fusion.40
  191.2 0.7 maximum_bitcast_fusion
  (53 shorter events, 5.3 us)
Async XLA Ops:
  7.2 10.5 %copy-start = (bf16[3,128,640]{2,1,0:T(8,128)(2,1)S(1)}, bf16[3,128,640]{2,1,0:T(8,128)(2,1)}, u32[]{:S(2)}) copy-start(bf16[3,128,640]{2,1,0:T(8,128)(2,1)} %param.7) | copy-start | bytes 1474564
  7.2 10.5 %copy-start.5 = (bf16[640,128]{1,0:T(8,128)(2,1)S(1)}, bf16[640,128]{1,0:T(8,128)(2,1)}, u32[]{:S(2)}) copy-start(bf16[640,128]{1,0:T(8,128)(2,1)} %param.8) | copy-start | bytes 491524
  7.2 92.9 %all-gather.3.cloned.1.call-start = ((), (), s32[]{:S(2)}) async-start(), calls=%async_computation.4 | async-start | bytes 4177920 | tf_op jit(solution)/shard_map/all_gather | solution.py:188
  8.2 7.6 %collective-permute-start.1 = (bf16[20,1280]{1,0:T(8,128)(2,1)S(1)}, bf16[20,1280]{1,0:T(8,128)(2,1)S(1)}, u32[]{:S(2)}, u32[]{:S(2)}) collective-permute-start(bf16[20,1280]{1,0:T(8,128)(2,1)S(1)} %get-tuple-element.31), channel_id=1, source_target_pairs={{0,256},{256,0},{1,257},{257,1},{2,258},{258,2},{3,259},{259,3},{4... | collective-permute-start | bytes 153608 | tf_op jit(solution)/shard_map/ppermute | solution.py:180
  17.6 1.8 copy-start.6
  17.7 163.2 %reduce-scatter.2.cloned.1.call-start = ((), (), s32[]{:S(2)}) async-start(), calls=%async_computation.3 | async-start | bytes 2785280 | tf_op jit(solution)/shard_map/reduce_scatter | solution.py:224
  42.2 3.2 %copy-start.9 = (f32[1,2,16]{2,1,0:T(2,128)S(1)}, f32[1,2,16]{2,1,0:T(2,128)}, u32[]{:S(2)}) copy-start(f32[1,2,16]{2,1,0:T(2,128)} %param.11) | copy-start | bytes 388
  43.2 27.4 %collective-permute-start = (bf16[2,384,640]{2,1,0:T(8,128)(2,1)}, bf16[2,384,640]{2,1,0:T(8,128)(2,1)S(1)}, u32[]{:S(2)}, u32[]{:S(2)}) collective-permute-start(bf16[2,384,640]{2,1,0:T(8,128)(2,1)} %bitcast.6), channel_id=1, source_target_pairs={{0,256},{256,0},{1,257},{257,1},{2,258},{258,2},{3,259},{259,3},{4... | collective-permute-start | bytes 2949128 | tf_op jit(solution)/shard_map/ppermute | solution.py:203
  70.7 1.6 copy-start.2
  117.9 22.5 %copy-start.4 = (f32[384,640]{1,0:T(8,128)S(1)}, f32[384,640]{1,0:T(8,128)}, u32[]{:S(2)}) copy-start(f32[384,640]{1,0:T(8,128)} %get-tuple-element.14) | copy-start | bytes 2949124
  117.9 22.6 %copy-start.3 = (bf16[640,768]{1,0:T(8,128)(2,1)S(1)}, bf16[640,768]{1,0:T(8,128)(2,1)}, u32[]{:S(2)}) copy-start(bf16[640,768]{1,0:T(8,128)(2,1)} %constant.23.clone) | copy-start | bytes 2949124
  119.4 21.1 %copy-start.1 = (f32[384,768]{1,0:T(8,128)S(1)}, f32[384,768]{1,0:T(8,128)}, u32[]{:S(2)}) copy-start(f32[384,768]{1,0:T(8,128)} %get-tuple-element.17) | copy-start | bytes 3538948
  119.4 21.0 %collective-permute-start.2 = (bf16[384,1408]{1,0:T(8,128)(2,1)S(1)}, bf16[384,1408]{1,0:T(8,128)(2,1)S(1)}, u32[]{:S(2)}, u32[]{:S(2)}) collective-permute-start(bf16[384,1408]{1,0:T(8,128)(2,1)S(1)} %pad_maximum_fusion), channel_id=1, source_target_pairs={{0,256},{256,0},{1,257},{257,1},{2,258},{258,2},{3,259},{259,3},{4... | collective-permute-start | bytes 3244040 | tf_op jit(solution)/shard_map/ppermute | solution.py:212
  142.2 19.3 %all-to-all-start.1 = ((bf16[16,2,3,8,640]{4,3,2,1,0:T(8,128)(2,1)}), bf16[16,2,3,8,640]{4,3,2,1,0:T(8,128)(2,1)S(1)}, u32[]{:S(2)}, u32[]{:S(2)}) async-start(bf16[16,2,3,8,640]{4,3,2,1,0:T(8,128)(2,1)} %pad_maximum_fusion.3), calls=%async_computation.1 | async-start | bytes 1966080 | tf_op jit(solution)/shard_map/all_to_all | solution.py:221
  161.5 0.9 copy-start.8
  180.8 10.3 %copy-start.7 = (bf16[64,1280]{1,0:T(8,128)(2,1)S(1)}, bf16[64,1280]{1,0:T(8,128)(2,1)}, u32[]{:S(2)}) copy-start(bf16[64,1280]{1,0:T(8,128)(2,1)} %reduce-scatter.2.cloned.1.call-done) | copy-start | bytes 491524
  181.9 7.6 %collective-permute-start.3 = (bf16[21,1280]{1,0:T(8,128)(2,1)S(1)}, bf16[21,1280]{1,0:T(8,128)(2,1)S(1)}, u32[]{:S(2)}, u32[]{:S(2)}) collective-permute-start(bf16[21,1280]{1,0:T(8,128)(2,1)S(1)} %pad_maximum_fusion.7), channel_id=1, source_target_pairs={{0,256},{256,0},{1,257},{257,1},{2,258},{258,2},{3,259},{259,3},{4... | collective-permute-start | bytes 161288 | tf_op jit(solution)/shard_map/ppermute | solution.py:228
Sparse Core Ops, SparseCore 0:
  17.8 82.2 all-gather.2
  109.5 71.2 reduce-scatter.1

commit v4 on v3

--- a/solution.py
+++ b/solution.py
@@ -15,7 +15,9 @@
 C1 = 0.044715
 
 
-def hidden_kernel(scale_ref, rows_ref, grad_ref, w_in_ref, w_out_ref, dw_ref, hidden_ref, dpre_ref):
+def hidden_kernel(
+    scale_ref, rows_ref, turned_ref, grad_ref, w_in_ref, w_out_ref, dw_ref, hidden_ref, dpre_ref
+):
     scale_in = scale_ref[0]
     scale_out = scale_ref[1]
     rows = rows_ref[...]
@@ -34,14 +36,14 @@
     slope = half + (0.5 * C0) * pre * (1.0 - tanh * tanh) * (1.0 + (3.0 * C1) * square)
     d_pre = (slope * d_hidden).astype(jnp.bfloat16)
     dpre_ref[...] = d_pre
-    dw = lax.dot_general(rows, d_pre, (((0,), (0,)), ((), ())), preferred_element_type=jnp.float32)
+    dw = jnp.dot(turned_ref[...], d_pre, preferred_element_type=jnp.float32)
     dw = (dw * scale_in).astype(dw_ref.dtype)
     for z in range(dw.shape[0] // PAD):
         dw_ref[z * STRIDE : z * STRIDE + PAD] = dw[z * PAD : (z + 1) * PAD]
         dw_ref[z * STRIDE + PAD : (z + 1) * STRIDE] = jnp.zeros((STRIDE - PAD, CHUNK), dw_ref.dtype)
 
 
-def hidden_of(scales, rows, grads, weights):
+def hidden_of(scales, rows, turned, grads, weights):
     count, depth = rows.shape
     width = grads.shape[1]
     zs = weights.shape[0]
@@ -53,6 +55,7 @@
         in_specs=[
             pl.BlockSpec(memory_space=pltpu.SMEM),
             pl.BlockSpec((count, depth), lambda r: (0, 0)),
+            pl.BlockSpec((depth, count), lambda r: (0, 0)),
             pl.BlockSpec((count, width), lambda r: (0, 0)),
             pl.BlockSpec((zs, PAD, CHUNK), lambda r: (0, 2 + r, 0)),
             pl.BlockSpec((zs // 2, 80, width), lambda r: (r, 0, 0)),
@@ -69,7 +72,7 @@
             bytes_accessed=16 * 1024 * 1024,
             transcendentals=count * chunks * CHUNK,
         ),
-    )(scales, rows, grads, weights, weights)
+    )(scales, rows, turned, grads, weights, weights)
 
 
 def rows_kernel(
@@ -204,9 +207,12 @@
     rows = jnp.concatenate([routed[0], twin[0]], 0)
     grads = jnp.concatenate([routed[1], twin[1]], 0)
     spread = jnp.asarray(placement(width, zs), bf16)
+    turned = lax.dot_general(
+        spread, rows, (((0,), (1,)), ((), ())), preferred_element_type=f32
+    ).astype(bf16)
     rows = jnp.dot(rows, spread, preferred_element_type=f32).astype(bf16)
 
-    dw, hidden, dpre = hidden_of(scales, rows, grads, weights)
+    dw, hidden, dpre = hidden_of(scales, rows, turned, grads, weights)
 
     out_own, drow_own, out_sent, drow_sent, peaks = rows_of(scales, hidden, dpre, weights, rows.shape[1])
     fetched = lax.ppermute(jnp.concatenate([out_sent, drow_sent], 1), "yh", SWAP)

time: 200 us -> 200 us (level)
  the two profiles are of different devices: /device:TPU:2 before, /device:TPU:22 now
where the time goes in v4:
time: 200 us; the launch traced here: 199 us
  waiting for transfers between devices  104 us (52%)
  blocking collectives  18.8 us (9%)
  Pallas kernels  18.2 us (9%)
  starting transfers between devices  17.5 us (9%)
  between operations  14.3 us (7%)
  other arithmetic  13.6 us (7%)
  matrix products  8.08 us (4%)
  local copies, waits for them, and re-layouts  4.46 us (2%)
    all_gather x1, waiting for transfers between devices, body(): weights = lax.all_gather(block, 'z', axis=0, tiled=False)  28.7 us
    ppermute x1, waiting for transfers between devices, body(): twin = lax.ppermute(routed, 'yh', SWAP)  20.8 us
    all_to_all x1, blocking collectives, body(): lax.all_to_all(both, along, split_axis=0, concat_axis=0, tiled=True)  18.8 us
    ppermute x1, waiting for transfers between devices, body(): lax.ppermute(jnp.concatenate([out_sent, drow_sent], 1), 'yh', SWAP)  18.1 us
    reduce_scatter x1, waiting for transfers between devices, body(): part = lax.psum_scatter(dw, 'z', scatter_dimension=0, tiled=True)  14.8 us
    all_to_all x1, waiting for transfers between devices, body(): lax.all_to_all(back, along, split_axis=0, concat_axis=0, tiled=True)  12.7 us
    pallas_call x1, Pallas kernels, hidden_of(): pl.pallas_call(hidden_kernel, grid=(chunks,), in_specs=[pl.BlockSpec(memo...  9.69 us
    pallas_call x1, Pallas kernels, rows_of(): pl.pallas_call(rows_kernel, grid=(chunks,), in_specs=[pl.BlockSpec(memory...  8.49 us
  transfers between devices with their start and end apart: 7, of which 7 were waited for; matrix products, arithmetic and copies ran while one was open for 10% of the time, Pallas kernels for 4%

profile of v4, /device:TPU:22, one launch (start us, length us, event | category | flops | bytes accessed | tf_op | source)
XLA Modules:
  0.0 199.4 jit_solution(8155956950258638763)
XLA Ops:
  7.2 0.9 broadcast_select_fusion.5
  8.2 2.2 %collective-permute-start.1 = (bf16[20,1280]{1,0:T(8,128)(2,1)S(1)}, bf16[20,1280]{1,0:T(8,128)(2,1)S(1)}, u32[]{:S(2)}, u32[]{:S(2)}) collective-permute-start(bf16[20,1280]{1,0:T(8,128)(2,1)S(1)} %get-tuple-element.31), channel_id=1, source_target_pairs={{0,256},{256,0},{1,257},{257,1},{2,258},{258,2},{3,259},{259,3},{4... | collective-permute-start | bytes 153608 | tf_op jit(solution)/shard_map/ppermute | solution.py:183
  10.6 5.2 %collective-permute-done.1 = bf16[20,1280]{1,0:T(8,128)(2,1)S(1)} collective-permute-done((bf16[20,1280]{1,0:T(8,128)(2,1)S(1)}, bf16[20,1280]{1,0:T(8,128)(2,1)S(1)}, u32[]{:S(2)}, u32[]{:S(2)}) %collective-permute-start.1) | collective-permute-done | bytes 51232 | tf_op jit(solution)/shard_map/ppermute | solution.py:183
  15.9 1.7 pad_maximum_fusion.4
  18.0 0.7 fusion.46
  19.1 0.8 fusion.45
  20.0 0.9 fusion.6
  21.0 18.8 %all_to_all.10 = bf16[16,2,3,8,640]{4,3,2,1,0:T(8,128)(2,1)S(1)} all-to-all(bf16[16,2,3,8,640]{4,3,2,1,0:T(8,128)(2,1)S(1)} %copy_bitcast_fusion), channel_id=1, replica_groups=mesh['yh'=2,'z'=16,'x'=4,'yl'=2,'c'=2] {'x','yl','c'}, dimensions={0} | all-to-all | bytes 1966080 | tf_op jit(solution)/shard_map/all_to_all | solution.py:204
  39.8 1.0 copy.25
  40.8 5.3 %collective-permute-start = (bf16[2,384,640]{2,1,0:T(8,128)(2,1)}, bf16[2,384,640]{2,1,0:T(8,128)(2,1)S(1)}, u32[]{:S(2)}, u32[]{:S(2)}) collective-permute-start(bf16[2,384,640]{2,1,0:T(8,128)(2,1)} %bitcast.6), channel_id=1, source_target_pairs={{0,256},{256,0},{1,257},{257,1},{2,258},{258,2},{3,259},{259,3},{4... | collective-permute-start | bytes 2949128 | tf_op jit(solution)/shard_map/ppermute | solution.py:206
  46.9 20.8 %collective-permute-done = bf16[2,384,640]{2,1,0:T(8,128)(2,1)S(1)} collective-permute-done((bf16[2,384,640]{2,1,0:T(8,128)(2,1)}, bf16[2,384,640]{2,1,0:T(8,128)(2,1)S(1)}, u32[]{:S(2)}, u32[]{:S(2)}) %collective-permute-start) | collective-permute-done | bytes 983072 | tf_op jit(solution)/shard_map/ppermute | solution.py:206
  67.7 1.2 convolution_convert_fusion
  68.9 1.5 copy.27.rows_ref
  70.4 1.1 pad_maximum_fusion.2.grad_ref
  71.5 28.7 %all-gather.3.cloned.1.call-done = bf16[3072,640]{1,0:T(8,128)(2,1)} async-done(((bf16[192,640]{1,0:T(8,128)(2,1)}), bf16[3072,640]{1,0:T(8,128)(2,1)}) %all-gather.3.cloned.1.call-update) | async-done | bytes 3932176 | tf_op jit(solution)/shard_map/all_gather | solution.py:191
  100.1 9.7 %shard_map.102 = (bf16[1024,1280]{1,0:T(8,128)(2,1)}, bf16[768,1280]{1,0:T(8,128)(2,1)}, bf16[768,1280]{1,0:T(8,128)(2,1)}) custom-call(f32[2]{0:T(128)} %broadcast_multiply_fusion.scale_ref, bf16[768,768]{1,0:T(8,128)(2,1)} %copy.27.rows_ref, bf16[768,768]{1,0:T(8,128)(2,1)} %bitcast.85, bf16[768,640]{1,0:T(8,128)(2,1)} %pad_maximum_fusion.2.grad_ref, ...), custom_call_target="tpu_custom_call" | custom-call | flops 3774873600 | bytes 16777216 | tf_op jit(solution)/shard_map/pallas_call | solution.py:52
  109.9 8.5 %shard_map.103 = (f32[384,640]{1,0:T(8,128)}, f32[384,768]{1,0:T(8,128)}, bf16[384,640]{1,0:T(8,128)(2,1)}, bf16[384,768]{1,0:T(8,128)(2,1)}, f32[8,1280]{1,0:T(8,128)}) custom-call(f32[2]{0:T(128)} %broadcast_multiply_fusion.scale_ref, bf16[768,1280]{1,0:T(8,128)(2,1)} %get-tuple-element.12.hidden_ref, bf16[768,1280]{1,0:T(8,128)(2,1)} %get-tuple-element.13.dpre_ref, ...), custom_call_target="tpu_custom_call" | custom-call | flops 2516582400 | bytes 16777216 | tf_op jit(solution)/shard_map/pallas_call | solution.py:121
  118.4 1.4 pad_maximum_fusion
  119.8 2.2 %collective-permute-start.2 = (bf16[384,1408]{1,0:T(8,128)(2,1)S(1)}, bf16[384,1408]{1,0:T(8,128)(2,1)S(1)}, u32[]{:S(2)}, u32[]{:S(2)}) collective-permute-start(bf16[384,1408]{1,0:T(8,128)(2,1)S(1)} %pad_maximum_fusion), channel_id=1, source_target_pairs={{0,256},{256,0},{1,257},{257,1},{2,258},{258,2},{3,259},{259,3},{4... | collective-permute-start | bytes 3244040 | tf_op jit(solution)/shard_map/ppermute | solution.py:218
  122.1 18.1 %collective-permute-done.2 = bf16[384,1408]{1,0:T(8,128)(2,1)S(1)} collective-permute-done((bf16[384,1408]{1,0:T(8,128)(2,1)S(1)}, bf16[384,1408]{1,0:T(8,128)(2,1)S(1)}, u32[]{:S(2)}, u32[]{:S(2)}) %collective-permute-start.2) | collective-permute-done | bytes 1081376 | tf_op jit(solution)/shard_map/ppermute | solution.py:218
  140.9 1.1 pad_maximum_fusion.3
  142.0 5.8 %all-to-all-start.1 = ((bf16[16,2,3,8,640]{4,3,2,1,0:T(8,128)(2,1)}), bf16[16,2,3,8,640]{4,3,2,1,0:T(8,128)(2,1)S(1)}, u32[]{:S(2)}, u32[]{:S(2)}) async-start(bf16[16,2,3,8,640]{4,3,2,1,0:T(8,128)(2,1)} %pad_maximum_fusion.3), calls=%async_computation.1 | async-start | bytes 1966080 | tf_op jit(solution)/shard_map/all_to_all | solution.py:227
  147.8 0.8 slice.144
  148.6 12.7 %all-to-all-done.1 = bf16[16,2,3,8,640]{4,3,2,1,0:T(8,128)(2,1)S(1)} async-done(((bf16[16,2,3,8,640]{4,3,2,1,0:T(8,128)(2,1)}), bf16[16,2,3,8,640]{4,3,2,1,0:T(8,128)(2,1)S(1)}, u32[]{:S(2)}, u32[]{:S(2)}) %all-to-all-start.1) | async-done | bytes 983072 | tf_op jit(solution)/shard_map/all_to_all | solution.py:227
  162.3 1.6 fusion.13
  164.6 2.1 %fusion.4 = bf16[3,128,640]{2,1,0:T(8,128)(2,1)} fusion(f32[3,128,640]{2,1,0:T(8,128)S(1)} %fusion.22, f32[3,128,128]{2,1,0:T(8,128)S(1)} %fusion.13, f32[3,128,128]{2,1,0:T(8,128)S(1)} %convolution_bitcast_fusion.1, bf16[640,128]{1,0:T(8,128)(2,1)S(1)} %copy-done.6, f32[3,128,128]{2,1,0:T(8,128)} %get-tuple-element.39, f32[3,128]{1,0:T(4,128)S(1)} %get-tuple-element.38), kind=kOutput, calls=%fused_computation.6 | convolution fusion | flops 63750656 | bytes 2229760 | tf_op jit(solution)/shard_map/bps,ds->bpd/dot_general | solution.py:252
  166.7 14.8 %reduce-scatter.2.cloned.1.call-done = bf16[64,1280]{1,0:T(8,128)(2,1)} async-done(((bf16[1024,1280]{1,0:T(8,128)(2,1)}), bf16[64,1280]{1,0:T(8,128)(2,1)}) %reduce-scatter.2.cloned.1.call-update) | async-done | bytes 163856 | tf_op jit(solution)/shard_map/reduce_scatter | solution.py:230
  181.5 1.0 broadcast_select_fusion.2
  182.5 1.9 collective-permute-start.3
  184.5 1.6 convolution_convert_fusion.1
  186.1 4.1 %collective-permute-done.3 = bf16[21,1280]{1,0:T(8,128)(2,1)S(1)} collective-permute-done((bf16[21,1280]{1,0:T(8,128)(2,1)S(1)}, bf16[21,1280]{1,0:T(8,128)(2,1)S(1)}, u32[]{:S(2)}, u32[]{:S(2)}) %collective-permute-start.3) | collective-permute-done | bytes 53792 | tf_op jit(solution)/shard_map/ppermute | solution.py:234
  190.2 0.8 fusion.40
  (58 shorter events, 5.9 us)
Async XLA Ops:
  7.2 10.5 %copy-start = (bf16[3,128,640]{2,1,0:T(8,128)(2,1)S(1)}, bf16[3,128,640]{2,1,0:T(8,128)(2,1)}, u32[]{:S(2)}) copy-start(bf16[3,128,640]{2,1,0:T(8,128)(2,1)} %param.7) | copy-start | bytes 1474564
  7.2 10.5 %copy-start.6 = (bf16[640,128]{1,0:T(8,128)(2,1)S(1)}, bf16[640,128]{1,0:T(8,128)(2,1)}, u32[]{:S(2)}) copy-start(bf16[640,128]{1,0:T(8,128)(2,1)} %param.8) | copy-start | bytes 491524
  7.2 93.0 %all-gather.3.cloned.1.call-start = ((), (), s32[]{:S(2)}) async-start(), calls=%async_computation.4 | async-start | bytes 4177920 | tf_op jit(solution)/shard_map/all_gather | solution.py:191
  8.2 7.6 %collective-permute-start.1 = (bf16[20,1280]{1,0:T(8,128)(2,1)S(1)}, bf16[20,1280]{1,0:T(8,128)(2,1)S(1)}, u32[]{:S(2)}, u32[]{:S(2)}) collective-permute-start(bf16[20,1280]{1,0:T(8,128)(2,1)S(1)} %get-tuple-element.31), channel_id=1, source_target_pairs={{0,256},{256,0},{1,257},{257,1},{2,258},{258,2},{3,259},{259,3},{4... | collective-permute-start | bytes 153608 | tf_op jit(solution)/shard_map/ppermute | solution.py:183
  17.6 2.3 %copy-start.7 = (bf16[3,128,640]{2,1,0:T(8,128)(2,1)S(1)}, bf16[3,128,640]{2,1,0:T(8,128)(2,1)}, u32[]{:S(2)}) copy-start(bf16[3,128,640]{2,1,0:T(8,128)(2,1)} %param.12) | copy-start | bytes 1474564
  17.7 163.9 %reduce-scatter.2.cloned.1.call-start = ((), (), s32[]{:S(2)}) async-start(), calls=%async_computation.3 | async-start | bytes 2785280 | tf_op jit(solution)/shard_map/reduce_scatter | solution.py:230
  39.8 6.3 %copy-start.11 = (f32[1,2,16]{2,1,0:T(2,128)S(1)}, f32[1,2,16]{2,1,0:T(2,128)}, u32[]{:S(2)}) copy-start(f32[1,2,16]{2,1,0:T(2,128)} %param.11) | copy-start | bytes 388
  40.8 26.8 %collective-permute-start = (bf16[2,384,640]{2,1,0:T(8,128)(2,1)}, bf16[2,384,640]{2,1,0:T(8,128)(2,1)S(1)}, u32[]{:S(2)}, u32[]{:S(2)}) collective-permute-start(bf16[2,384,640]{2,1,0:T(8,128)(2,1)} %bitcast.6), channel_id=1, source_target_pairs={{0,256},{256,0},{1,257},{257,1},{2,258},{258,2},{3,259},{259,3},{4... | collective-permute-start | bytes 2949128 | tf_op jit(solution)/shard_map/ppermute | solution.py:206
  46.8 20.9 %copy-start.3 = (bf16[640,768]{1,0:T(8,128)(2,1)S(1)}, bf16[640,768]{1,0:T(8,128)(2,1)}, u32[]{:S(2)}) copy-start(bf16[640,768]{1,0:T(8,128)(2,1)} %constant.23.clone) | copy-start | bytes 2949124
  68.9 1.5 copy-start.2
  118.3 21.8 %copy-start.5 = (f32[384,640]{1,0:T(8,128)S(1)}, f32[384,640]{1,0:T(8,128)}, u32[]{:S(2)}) copy-start(f32[384,640]{1,0:T(8,128)} %get-tuple-element.14) | copy-start | bytes 2949124
  118.4 21.9 %copy-start.4 = (bf16[640,768]{1,0:T(8,128)(2,1)S(1)}, bf16[640,768]{1,0:T(8,128)(2,1)}, u32[]{:S(2)}) copy-start(bf16[640,768]{1,0:T(8,128)(2,1)} %constant.23.clone) | copy-start | bytes 2949124
  119.8 20.4 %copy-start.1 = (f32[384,768]{1,0:T(8,128)S(1)}, f32[384,768]{1,0:T(8,128)}, u32[]{:S(2)}) copy-start(f32[384,768]{1,0:T(8,128)} %get-tuple-element.17) | copy-start | bytes 3538948
  119.8 20.3 %collective-permute-start.2 = (bf16[384,1408]{1,0:T(8,128)(2,1)S(1)}, bf16[384,1408]{1,0:T(8,128)(2,1)S(1)}, u32[]{:S(2)}, u32[]{:S(2)}) collective-permute-start(bf16[384,1408]{1,0:T(8,128)(2,1)S(1)} %pad_maximum_fusion), channel_id=1, source_target_pairs={{0,256},{256,0},{1,257},{257,1},{2,258},{258,2},{3,259},{259,3},{4... | collective-permute-start | bytes 3244040 | tf_op jit(solution)/shard_map/ppermute | solution.py:218
  142.0 19.4 %all-to-all-start.1 = ((bf16[16,2,3,8,640]{4,3,2,1,0:T(8,128)(2,1)}), bf16[16,2,3,8,640]{4,3,2,1,0:T(8,128)(2,1)S(1)}, u32[]{:S(2)}, u32[]{:S(2)}) async-start(bf16[16,2,3,8,640]{4,3,2,1,0:T(8,128)(2,1)} %pad_maximum_fusion.3), calls=%async_computation.1 | async-start | bytes 1966080 | tf_op jit(solution)/shard_map/all_to_all | solution.py:227
  147.8 13.7 %copy-start.8 = (bf16[3,128,640]{2,1,0:T(8,128)(2,1)S(1)}, bf16[3,128,640]{2,1,0:T(8,128)(2,1)}, u32[]{:S(2)}) copy-start(bf16[3,128,640]{2,1,0:T(8,128)(2,1)} %param.12) | copy-start | bytes 1474564
  161.4 0.9 copy-start.10
  181.5 10.3 %copy-start.9 = (bf16[64,1280]{1,0:T(8,128)(2,1)S(1)}, bf16[64,1280]{1,0:T(8,128)(2,1)}, u32[]{:S(2)}) copy-start(bf16[64,1280]{1,0:T(8,128)(2,1)} %reduce-scatter.2.cloned.1.call-done) | copy-start | bytes 491524
  182.5 7.6 %collective-permute-start.3 = (bf16[21,1280]{1,0:T(8,128)(2,1)S(1)}, bf16[21,1280]{1,0:T(8,128)(2,1)S(1)}, u32[]{:S(2)}, u32[]{:S(2)}) collective-permute-start(bf16[21,1280]{1,0:T(8,128)(2,1)S(1)} %pad_maximum_fusion.7), channel_id=1, source_target_pairs={{0,256},{256,0},{1,257},{257,1},{2,258},{258,2},{3,259},{259,3},{4... | collective-permute-start | bytes 161288 | tf_op jit(solution)/shard_map/ppermute | solution.py:234
Sparse Core Ops, SparseCore 0:
  17.8 82.3 all-gather.2
  110.0 71.4 reduce-scatter.1
